TPU v7x, 32 devices: a whole 2x2x4 slice. The times are simulated.
32 devices in a mesh: row: 8 (over z, y), col: 4 (over x, core).
Axes of the slice: x: 2, y: 2, z: 4, core: 2. Of those that a mesh axis runs over, the one named last changes fastest.
Arguments:
- lower: float32 [6, 2048, 2048], P(None, 'row', 'col'), may hold values from -0.046875 to 0.046875
- dinv: float32 [4, 2048, 2048], P(None, 'row', 'col'), as said below
- kcols: float32 [4, 2048, 2048], P(None, 'row', 'col'), may hold values from -6 to 6
- prior: float32 [2048], P('col'), may hold values from 3 to 5
Outputs:
- solved_columns: float32 [4, 2048, 2048], P(None, 'row', 'col')
- variance: float32 [2048], P('col')
Inputs may be any that keep to these rules, and one draw needn't show every extreme that they name: Each block of dinv is lower triangular with a positive diagonal.
All inputs are finite; a program needn't handle non-finite values.
Results may differ from a plain program's by a relative error of at most 0.0001.
Values sent between devices are 32-bit elements; how exact they have to be, the bound alone decides.
No kernel may reach another device: no remote copies, remote signals or barrier semaphores. Data moves between devices by JAX's collectives and lax.ppermute only.
A program may use at most 64 MiB of HBM per device.

v0:
```python
import functools

import jax
import jax.numpy as jnp
from jax import lax
from jax.experimental import pallas as pl
from jax.experimental.pallas import tpu as pltpu
from jax.sharding import PartitionSpec as P

STREAMS = 2
LAYERS = 4
dot = functools.partial(jnp.dot, preferred_element_type=jnp.float32)


def halves(value):
    high = value.astype(jnp.bfloat16)
    return high, (value - high.astype(jnp.float32)).astype(jnp.bfloat16)


def product_kernel(layers, sign, by_xor, pieces, based, *refs):
    factor, panels, refs = refs[:pieces], refs[pieces : pieces + layers], refs[pieces + layers :]
    bases, (own, away, fh, fl, xh, xl) = refs[:-6], refs[-6:]
    height = panels[0].shape[0]
    layer = lax.axis_index("row") // 2
    column = lax.axis_index("col")
    for hop, ref in enumerate(panels):
        source = lax.rem(layer + layers - hop, layers)
        slot = jnp.bitwise_xor(source, column) if by_xor else source
        start = pl.multiple_of(slot * height, height)
        xh[pl.ds(start, height), :], xl[pl.ds(start, height), :] = halves(ref[...])
    for half, out in ((1, away), (0, own)):
        for slot in range(layers):
            block = factor[slot][half] if pieces > 1 else factor[0][slot, 0, half]
            section = slice(slot * height, (slot + 1) * height)
            fh[:, section], fl[:, section] = halves(block)
        total = dot(fl[...], xh[...]) + dot(fh[...], xl[...]) + dot(fh[...], xh[...])
        total = total if sign > 0 else -total
        out[...] = bases[half][...] + total if based[half] else total


def after(value, *events):
    return lax.optimization_barrier((value, *events))[0]


def make_body(rows, cols, streams):
    layers = rows // 2
    pair = [(r, r ^ 1) for r in range(rows)]

    ring = [(r, (r + 2) % rows) for r in range(rows)]

    def body(lower, dinv, kcols, prior):
        segments, height, breadth = kcols.shape
        observed = segments * height * rows
        width = breadth // streams
        layer, parity = lax.axis_index("row") // 2, lax.axis_index("row") % 2
        column = lax.axis_index("col")
        vmem = functools.partial(pltpu.CompilerParams, vmem_limit_bytes=24 * 2**20)

        def swap(value):
            return lax.ppermute(value, "row", pair)

        def cross(value, bits):
            return lax.ppermute(value, "col", [(c, c ^ bits) for c in range(cols)])

        def by_parity(blocks):
            even, odd = blocks[..., :height], blocks[..., height:]
            return jnp.where(parity == 0, even, odd), jnp.where(parity == 0, odd, even)

        def ring_of(panels, waits={}):
            slots = [[panel] for panel in panels]
            for hop in range(1, layers):
                for i in range(streams):
                    value = slots[i][-1]
                    if (i, hop) in waits:
                        value = after(value, *waits[i, hop])
                    slots[i].append(lax.ppermute(value, "row", ring))
            return slots, [[stream[hop] for stream in slots] for hop in range(layers)]

        def block_spec(shape):
            return pl.BlockSpec(shape, lambda i: (0,) * len(shape))

        def product(factor, panels, bases=(), sign=1):
            if isinstance(factor, list):
                pieces, specs = factor, [block_spec(piece.shape) for piece in factor]
            else:
                pieces, index = [factor[0]], factor[1]
                specs = [pl.BlockSpec((cols, 1, 2, height, height), lambda i: (0, index, 0, 0, 0))]
            wide = panels[0].shape[1]
            depth = layers * height
            shape = jax.ShapeDtypeStruct((height, wide), jnp.float32)
            based = (len(bases) > 0, len(bases) > 1)
            return pl.pallas_call(
                functools.partial(product_kernel, layers, sign, len(pieces) > 1, len(pieces), based),
                grid=(1,),
                out_shape=[shape] * 2,
                in_specs=specs + [block_spec((height, wide))] * (layers + len(bases)),
                out_specs=[block_spec((height, wide))] * 2,
                scratch_shapes=[pltpu.VMEM((height, depth), jnp.bfloat16)] * 2
                + [pltpu.VMEM((depth, wide), jnp.bfloat16)] * 2,
                compiler_params=pltpu.CompilerParams(vmem_limit_bytes=24 * 2**20),
                cost_estimate=pl.CostEstimate(
                    flops=12 * height * depth * wide,
                    bytes_accessed=4 * (2 * height * depth + (layers + 2 + len(bases)) * height * wide),
                    transcendentals=0,
                ),
            )(*pieces, *panels, *bases)

        cut = [slice(i * width, (i + 1) * width) for i in range(streams)]
        sums = [[(kcols[s, :, c],) for s in range(segments)] for c in cut]
        solved = [[None] * segments for i in range(streams)]

        def block(s, t):
            return dinv[s] if s == t else lower[s * (s - 1) // 2 + t]

        def exchange(keys, start, use):
            mine, theirs = by_parity(jnp.stack([block(s, t) for s, t in keys]))
            got = swap(after(theirs, *start) if start else theirs)
            return jnp.stack([mine, after(got, *use)], axis=-3), got

        found = {}

        def fetch(keys, start, use):
            piece, got = exchange(keys, start, use)
            whole = lax.all_gather(piece, "col", axis=0)
            for index, key in enumerate(keys):
                found[key] = (whole, index)

        firsts = [kcols[0, :, c] for c in cut]
        one = lax.ppermute(firsts[0], "row", ring)
        piece, got = exchange([(0, 0)], [], [one])
        near = cross(piece[0], 1)
        beside = cross(piece[0], 2)
        far = cross(after(beside, near), 1)
        found[0, 0] = [piece[0], near, beside, far]
        slots, hops = ring_of(firsts, {(streams - 1, 2): [near], (streams - 1, 3): [far]})
        fetch([(1, 0)], [got], hops[2])
        fetch([(1, 1), (2, 0), (2, 1)], [got, *hops[2]], hops[3])
        for s in range(segments):
            for i in range(streams):
                own, away = product(found[s, s], slots[i])
                solved[i][s] = own + swap(away)
            if s + 1 == segments:
                break
            panels, after_x = ring_of([solved[i][s] for i in range(streams)])
            if s == 0:
                fetch([(2, 2), (3, 0), (3, 1), (3, 2), (3, 3)], after_x[0], after_x[3])
            residuals = []
            for i in range(streams):
                own, away = product(found[s + 1, s], panels[i], sums[i][s + 1], -1)
                residuals.append(own + swap(away))
            early = []
            if s == 0:
                for i in range(streams):
                    sums[i][2] = product(found[2, 0], panels[i], sums[i][2], -1)
                    early.append(sums[i][2][0])
            if s == 1:
                for i in range(streams):
                    sums[i][3] = product(found[3, 0], first_panels[i], sums[i][3], -1)
                    sums[i][3] = product(found[3, 1], panels[i], sums[i][3], -1)
                    early.append(sums[i][3][0])
            first_panels = panels
            slots, hops = ring_of(residuals, {(streams - 1, 3): early} if early else {})
        solution = jnp.stack(
            [jnp.concatenate([solved[i][s] for i in range(streams)], axis=1) for s in range(segments)]
        )
        totals = jnp.sum(solution * solution, axis=(0, 1))
        bit = 1
        while bit < rows:
            totals = totals + lax.ppermute(totals, "row", [(r, r ^ bit) for r in range(rows)])
            bit *= 2
        variance = prior - totals / observed
        return (solution, variance)

    return body


def whole_body(lower, dinv, kcols, prior):
    segments = kcols.shape[0]
    high = functools.partial(dot, precision=lax.Precision.HIGHEST)
    spread, solved = [], []
    for s in range(segments):
        residual = kcols[s]
        for t in range(s):
            block = lax.all_gather(lower[s * (s - 1) // 2 + t], "col", axis=1, tiled=True)
            residual = residual - high(block, spread[t])
        whole = lax.all_gather(residual, "row", axis=0, tiled=True)
        answer = high(lax.all_gather(dinv[s], "col", axis=1, tiled=True), whole)
        solved.append(answer)
        if s + 1 < segments:
            spread.append(lax.all_gather(answer, "row", axis=0, tiled=True))
    solution = jnp.stack(solved)
    totals = lax.psum(jnp.sum(solution * solution, axis=(0, 1)), "row")
    return solution, prior - totals / (segments * dinv.shape[2] * lax.axis_size("col"))


def solution(mesh):
    rows, cols = mesh.shape["row"], mesh.shape["col"]
    if rows == 2 * LAYERS and cols == LAYERS:
        body = make_body(rows, cols, STREAMS)
    else:
        body = whole_body
    in_specs = (P(None, "row", "col"), P(None, "row", "col"), P(None, "row", "col"), P("col"))
    out_specs = (P(None, "row", "col"), P("col"))
    return jax.shard_map(body, mesh=mesh, in_specs=in_specs, out_specs=out_specs, check_vma=False)
```

profile of v0, /device:TPU:0, one launch (start us, length us, event | category | flops | bytes accessed | tf_op | source)
XLA Modules:
  0.0 382.0 jit_solution(2158539144298837489)
XLA Ops:
  8.3 3.0 collective-permute-start
  17.6 5.8 %collective-permute-done.1.refs_5_ = f32[256,256]{1,0:T(8,128)S(1)} collective-permute-done((f32[256,256]{1,0:T(8,128)S(1)}, f32[256,256]{1,0:T(8,128)S(1)}, u32[]{:S(2)}, u32[]{:S(2)}) %collective-permute-start.1) | collective-permute-done | bytes 262176 | tf_op jit(solution)/shard_map/ppermute | solution.py:129
  25.7 8.8 %collective-permute-done.8.refs_5_ = f32[256,256]{1,0:T(8,128)S(1)} collective-permute-done((f32[256,256]{1,0:T(8,128)S(1)}, f32[256,256]{1,0:T(8,128)S(1)}, u32[]{:S(2)}, u32[]{:S(2)}) %collective-permute-start.8) | collective-permute-done | bytes 262176 | tf_op jit(solution)/shard_map/ppermute | solution.py:76
  34.6 5.6 %collective-permute-done.5.refs_6_ = f32[256,256]{1,0:T(8,128)S(1)} collective-permute-done((f32[256,256]{1,0:T(8,128)S(1)}, f32[256,256]{1,0:T(8,128)S(1)}, u32[]{:S(2)}, u32[]{:S(2)}) %collective-permute-start.5) | collective-permute-done | bytes 262176 | tf_op jit(solution)/shard_map/ppermute | solution.py:76
  40.2 5.2 %collective-permute-done.9.refs_6_ = f32[256,256]{1,0:T(8,128)S(1)} collective-permute-done((f32[256,256]{1,0:T(8,128)S(1)}, f32[256,256]{1,0:T(8,128)S(1)}, u32[]{:S(2)}, u32[]{:S(2)}) %collective-permute-start.9) | collective-permute-done | bytes 262176 | tf_op jit(solution)/shard_map/ppermute | solution.py:76
  49.7 17.9 %collective-permute-done.3.refs_2_ = f32[2,256,256]{2,1,0:T(8,128)S(1)} collective-permute-done((f32[2,256,256]{2,1,0:T(8,128)S(1)}, f32[2,256,256]{2,1,0:T(8,128)S(1)}, u32[]{:S(2)}, u32[]{:S(2)}) %collective-permute-start.3) | collective-permute-done | bytes 524320 | tf_op jit(solution)/shard_map/ppermute | solution.py:63
  69.5 9.1 %collective-permute-done.6.refs_7_ = f32[256,256]{1,0:T(8,128)S(1)} collective-permute-done((f32[256,256]{1,0:T(8,128)S(1)}, f32[256,256]{1,0:T(8,128)S(1)}, u32[]{:S(2)}, u32[]{:S(2)}) %collective-permute-start.6) | collective-permute-done | bytes 262176 | tf_op jit(solution)/shard_map/ppermute | solution.py:76
  79.3 4.5 %collective-permute-done.10.refs_7_ = f32[256,256]{1,0:T(8,128)S(1)} collective-permute-done((f32[256,256]{1,0:T(8,128)S(1)}, f32[256,256]{1,0:T(8,128)S(1)}, u32[]{:S(2)}, u32[]{:S(2)}) %collective-permute-start.10) | collective-permute-done | bytes 262176 | tf_op jit(solution)/shard_map/ppermute | solution.py:76
  84.4 3.1 collective-permute-done.12
  96.5 5.7 %collective-permute-done.7 = f32[256,256]{1,0:T(8,128)S(1)} collective-permute-done((f32[256,256]{1,0:T(8,128)S(1)}, f32[256,256]{1,0:T(8,128)S(1)}, u32[]{:S(2)}, u32[]{:S(2)}) %collective-permute-start.7) | collective-permute-done | bytes 262176 | tf_op jit(solution)/shard_map/ppermute | solution.py:60
  102.2 4.3 %collective-permute-done.11 = f32[256,256]{1,0:T(8,128)S(1)} collective-permute-done((f32[256,256]{1,0:T(8,128)S(1)}, f32[256,256]{1,0:T(8,128)S(1)}, u32[]{:S(2)}, u32[]{:S(2)}) %collective-permute-start.11) | collective-permute-done | bytes 262176 | tf_op jit(solution)/shard_map/ppermute | solution.py:60
  107.1 11.0 %collective-permute-done.14.refs_2_ = f32[256,256]{1,0:T(8,128)S(1)} collective-permute-done((f32[256,256]{1,0:T(8,128)S(1)}, f32[256,256]{1,0:T(8,128)S(1)}, u32[]{:S(2)}, u32[]{:S(2)}) %collective-permute-start.14) | collective-permute-done | bytes 262176 | tf_op jit(solution)/shard_map/ppermute | solution.py:76
  118.1 5.6 %collective-permute-done.22.refs_2_ = f32[256,256]{1,0:T(8,128)S(1)} collective-permute-done((f32[256,256]{1,0:T(8,128)S(1)}, f32[256,256]{1,0:T(8,128)S(1)}, u32[]{:S(2)}, u32[]{:S(2)}) %collective-permute-start.22) | collective-permute-done | bytes 262176 | tf_op jit(solution)/shard_map/ppermute | solution.py:76
  123.7 5.6 %collective-permute-done.15.refs_3_ = f32[256,256]{1,0:T(8,128)S(1)} collective-permute-done((f32[256,256]{1,0:T(8,128)S(1)}, f32[256,256]{1,0:T(8,128)S(1)}, u32[]{:S(2)}, u32[]{:S(2)}) %collective-permute-start.15) | collective-permute-done | bytes 262176 | tf_op jit(solution)/shard_map/ppermute | solution.py:76
  129.3 5.6 %collective-permute-done.23.refs_3_ = f32[256,256]{1,0:T(8,128)S(1)} collective-permute-done((f32[256,256]{1,0:T(8,128)S(1)}, f32[256,256]{1,0:T(8,128)S(1)}, u32[]{:S(2)}, u32[]{:S(2)}) %collective-permute-start.23) | collective-permute-done | bytes 262176 | tf_op jit(solution)/shard_map/ppermute | solution.py:76
  135.0 5.6 %collective-permute-done.16.refs_4_ = f32[256,256]{1,0:T(8,128)S(1)} collective-permute-done((f32[256,256]{1,0:T(8,128)S(1)}, f32[256,256]{1,0:T(8,128)S(1)}, u32[]{:S(2)}, u32[]{:S(2)}) %collective-permute-start.16) | collective-permute-done | bytes 262176 | tf_op jit(solution)/shard_map/ppermute | solution.py:76
  140.6 3.5 collective-permute-done.24.refs_4_
  152.8 5.8 %collective-permute-done.17 = f32[256,256]{1,0:T(8,128)S(1)} collective-permute-done((f32[256,256]{1,0:T(8,128)S(1)}, f32[256,256]{1,0:T(8,128)S(1)}, u32[]{:S(2)}, u32[]{:S(2)}) %collective-permute-start.17) | collective-permute-done | bytes 262176 | tf_op jit(solution)/shard_map/ppermute | solution.py:60
  161.5 8.1 %collective-permute-done.18.refs_2_ = f32[256,256]{1,0:T(8,128)S(1)} collective-permute-done((f32[256,256]{1,0:T(8,128)S(1)}, f32[256,256]{1,0:T(8,128)S(1)}, u32[]{:S(2)}, u32[]{:S(2)}) %collective-permute-start.18) | collective-permute-done | bytes 262176 | tf_op jit(solution)/shard_map/ppermute | solution.py:76
  170.3 5.0 %collective-permute-done.26.refs_2_ = f32[256,256]{1,0:T(8,128)} collective-permute-done((f32[256,256]{1,0:T(8,128)S(1)}, f32[256,256]{1,0:T(8,128)}, u32[]{:S(2)}, u32[]{:S(2)}) %collective-permute-start.26) | collective-permute-done | bytes 262176 | tf_op jit(solution)/shard_map/ppermute | solution.py:76
  175.3 5.6 %collective-permute-done.19.refs_3_ = f32[256,256]{1,0:T(8,128)} collective-permute-done((f32[256,256]{1,0:T(8,128)S(1)}, f32[256,256]{1,0:T(8,128)}, u32[]{:S(2)}, u32[]{:S(2)}) %collective-permute-start.19) | collective-permute-done | bytes 262176 | tf_op jit(solution)/shard_map/ppermute | solution.py:76
  181.0 3.4 copy.8
  187.0 4.1 %collective-permute-done.20.refs_4_ = f32[256,256]{1,0:T(8,128)} collective-permute-done((f32[256,256]{1,0:T(8,128)}, f32[256,256]{1,0:T(8,128)}, u32[]{:S(2)}, u32[]{:S(2)}) %collective-permute-start.20) | collective-permute-done | bytes 262176 | tf_op jit(solution)/shard_map/ppermute | solution.py:76
  200.8 3.4 collective-permute-done.29
  204.2 7.6 %collective-permute-done.31.refs_2_ = f32[256,256]{1,0:T(8,128)S(1)} collective-permute-done((f32[256,256]{1,0:T(8,128)S(1)}, f32[256,256]{1,0:T(8,128)S(1)}, u32[]{:S(2)}, u32[]{:S(2)}) %collective-permute-start.31) | collective-permute-done | bytes 262176 | tf_op jit(solution)/shard_map/ppermute | solution.py:76
  211.8 5.6 %collective-permute-done.39.refs_2_ = f32[256,256]{1,0:T(8,128)S(1)} collective-permute-done((f32[256,256]{1,0:T(8,128)S(1)}, f32[256,256]{1,0:T(8,128)S(1)}, u32[]{:S(2)}, u32[]{:S(2)}) %collective-permute-start.39) | collective-permute-done | bytes 262176 | tf_op jit(solution)/shard_map/ppermute | solution.py:76
  217.4 5.6 %collective-permute-done.32.refs_3_ = f32[256,256]{1,0:T(8,128)S(1)} collective-permute-done((f32[256,256]{1,0:T(8,128)S(1)}, f32[256,256]{1,0:T(8,128)S(1)}, u32[]{:S(2)}, u32[]{:S(2)}) %collective-permute-start.32) | collective-permute-done | bytes 262176 | tf_op jit(solution)/shard_map/ppermute | solution.py:76
  223.1 5.5 %collective-permute-done.40.refs_3_ = f32[256,256]{1,0:T(8,128)S(1)} collective-permute-done((f32[256,256]{1,0:T(8,128)S(1)}, f32[256,256]{1,0:T(8,128)S(1)}, u32[]{:S(2)}, u32[]{:S(2)}) %collective-permute-start.40) | collective-permute-done | bytes 262176 | tf_op jit(solution)/shard_map/ppermute | solution.py:76
  233.1 6.1 %collective-permute-done.41.refs_4_ = f32[256,256]{1,0:T(8,128)S(1)} collective-permute-done((f32[256,256]{1,0:T(8,128)S(1)}, f32[256,256]{1,0:T(8,128)S(1)}, u32[]{:S(2)}, u32[]{:S(2)}) %collective-permute-start.41) | collective-permute-done | bytes 262176 | tf_op jit(solution)/shard_map/ppermute | solution.py:76
  240.6 6.2 %collective-permute-done.42 = f32[256,256]{1,0:T(8,128)S(1)} collective-permute-done((f32[256,256]{1,0:T(8,128)S(1)}, f32[256,256]{1,0:T(8,128)S(1)}, u32[]{:S(2)}, u32[]{:S(2)}) %collective-permute-start.42) | collective-permute-done | bytes 262176 | tf_op jit(solution)/shard_map/ppermute | solution.py:60
  247.6 3.9 %collective-permute-done.35.refs_2_ = f32[256,256]{1,0:T(8,128)S(1)} collective-permute-done((f32[256,256]{1,0:T(8,128)S(1)}, f32[256,256]{1,0:T(8,128)S(1)}, u32[]{:S(2)}, u32[]{:S(2)}) %collective-permute-start.35) | collective-permute-done | bytes 262176 | tf_op jit(solution)/shard_map/ppermute | solution.py:76
  252.3 5.7 %collective-permute-done.43.refs_2_ = f32[256,256]{1,0:T(8,128)} collective-permute-done((f32[256,256]{1,0:T(8,128)S(1)}, f32[256,256]{1,0:T(8,128)}, u32[]{:S(2)}, u32[]{:S(2)}) %collective-permute-start.43) | collective-permute-done | bytes 262176 | tf_op jit(solution)/shard_map/ppermute | solution.py:76
  260.8 4.8 %copy.9 = f32[20,2,256,256]{3,2,1,0:T(8,128)S(1)} copy(f32[20,2,256,256]{3,2,0,1:T(8,128)} %all-gather.11.cloned.1.call-done) | data formatting | bytes 20971520 | tf_op jit(solution)/shard_map/all_gather | solution.py:124
  274.2 5.9 %collective-permute-done.45.refs_4_ = f32[256,256]{1,0:T(8,128)S(1)} collective-permute-done((f32[256,256]{1,0:T(8,128)}, f32[256,256]{1,0:T(8,128)S(1)}, u32[]{:S(2)}, u32[]{:S(2)}) %collective-permute-start.45) | collective-permute-done | bytes 262176 | tf_op jit(solution)/shard_map/ppermute | solution.py:76
  285.1 4.2 %collective-permute-done.46 = f32[256,256]{1,0:T(8,128)S(1)} collective-permute-done((f32[256,256]{1,0:T(8,128)S(1)}, f32[256,256]{1,0:T(8,128)S(1)}, u32[]{:S(2)}, u32[]{:S(2)}) %collective-permute-start.46) | collective-permute-done | bytes 262176 | tf_op jit(solution)/shard_map/ppermute | solution.py:60
  289.5 6.1 %collective-permute-done.47.refs_2_ = f32[256,256]{1,0:T(8,128)S(1)} collective-permute-done((f32[256,256]{1,0:T(8,128)S(1)}, f32[256,256]{1,0:T(8,128)S(1)}, u32[]{:S(2)}, u32[]{:S(2)}) %collective-permute-start.47) | collective-permute-done | bytes 262176 | tf_op jit(solution)/shard_map/ppermute | solution.py:76
  295.6 4.3 %collective-permute-done.55.refs_2_ = f32[256,256]{1,0:T(8,128)S(1)} collective-permute-done((f32[256,256]{1,0:T(8,128)S(1)}, f32[256,256]{1,0:T(8,128)S(1)}, u32[]{:S(2)}, u32[]{:S(2)}) %collective-permute-start.55) | collective-permute-done | bytes 262176 | tf_op jit(solution)/shard_map/ppermute | solution.py:76
  299.9 3.9 %collective-permute-done.48.refs_3_ = f32[256,256]{1,0:T(8,128)S(1)} collective-permute-done((f32[256,256]{1,0:T(8,128)S(1)}, f32[256,256]{1,0:T(8,128)S(1)}, u32[]{:S(2)}, u32[]{:S(2)}) %collective-permute-start.48) | collective-permute-done | bytes 262176 | tf_op jit(solution)/shard_map/ppermute | solution.py:76
  303.8 6.9 %collective-permute-done.56.refs_3_ = f32[256,256]{1,0:T(8,128)S(1)} collective-permute-done((f32[256,256]{1,0:T(8,128)S(1)}, f32[256,256]{1,0:T(8,128)S(1)}, u32[]{:S(2)}, u32[]{:S(2)}) %collective-permute-start.56) | collective-permute-done | bytes 262176 | tf_op jit(solution)/shard_map/ppermute | solution.py:76
  310.7 5.6 %collective-permute-done.49.refs_4_ = f32[256,256]{1,0:T(8,128)S(1)} collective-permute-done((f32[256,256]{1,0:T(8,128)S(1)}, f32[256,256]{1,0:T(8,128)S(1)}, u32[]{:S(2)}, u32[]{:S(2)}) %collective-permute-start.49) | collective-permute-done | bytes 262176 | tf_op jit(solution)/shard_map/ppermute | solution.py:76
  319.0 2.9 collective-permute-done.57.refs_4_
  324.7 4.7 %collective-permute-done.58 = f32[256,256]{1,0:T(8,128)S(1)} collective-permute-done((f32[256,256]{1,0:T(8,128)S(1)}, f32[256,256]{1,0:T(8,128)S(1)}, u32[]{:S(2)}, u32[]{:S(2)}) %collective-permute-start.58) | collective-permute-done | bytes 262176 | tf_op jit(solution)/shard_map/ppermute | solution.py:60
  329.5 5.3 %collective-permute-done.51.refs_2_ = f32[256,256]{1,0:T(8,128)S(1)} collective-permute-done((f32[256,256]{1,0:T(8,128)S(1)}, f32[256,256]{1,0:T(8,128)S(1)}, u32[]{:S(2)}, u32[]{:S(2)}) %collective-permute-start.51) | collective-permute-done | bytes 262176 | tf_op jit(solution)/shard_map/ppermute | solution.py:76
  334.8 2.9 collective-permute-done.59.refs_2_
  337.7 5.3 %collective-permute-done.52.refs_3_ = f32[256,256]{1,0:T(8,128)S(1)} collective-permute-done((f32[256,256]{1,0:T(8,128)S(1)}, f32[256,256]{1,0:T(8,128)S(1)}, u32[]{:S(2)}, u32[]{:S(2)}) %collective-permute-start.52) | collective-permute-done | bytes 262176 | tf_op jit(solution)/shard_map/ppermute | solution.py:76
  345.9 5.3 %collective-permute-done.53.refs_4_ = f32[256,256]{1,0:T(8,128)S(1)} collective-permute-done((f32[256,256]{1,0:T(8,128)S(1)}, f32[256,256]{1,0:T(8,128)S(1)}, u32[]{:S(2)}, u32[]{:S(2)}) %collective-permute-start.53) | collective-permute-done | bytes 262176 | tf_op jit(solution)/shard_map/ppermute | solution.py:76
  366.8 3.6 collective-permute-done.64
  370.4 4.5 %collective-permute-done.65 = f32[512]{0:T(512)S(1)} collective-permute-done((f32[512]{0:T(512)S(1)}, f32[512]{0:T(512)S(1)}, u32[]{:S(2)}, u32[]{:S(2)}) %collective-permute-start.65) | collective-permute-done | bytes 2080 | tf_op jit(solution)/shard_map/ppermute | solution.py:169
  (234 shorter events, 99.7 us)
Async XLA Ops:
  7.2 138.7 %all-gather.9.cloned.1.call-start = ((), (), s32[]{:S(2)}) async-start(), calls=%async_computation.1 | async-start | bytes 2621440 | tf_op jit(solution)/shard_map/all_gather | solution.py:124
  8.3 9.3 %collective-permute-start = (f32[1,256,256]{2,1,0:T(8,128)S(1)}, f32[1,256,256]{2,1,0:T(8,128)S(1)}, u32[]{:S(2)}, u32[]{:S(2)}) collective-permute-start(f32[1,256,256]{2,1,0:T(8,128)S(1)} %get-tuple-element.124), channel_id=1, source_target_pairs={{0,4},{4,0},{8,12},{12,8},{16,20},{20,16},{24,28},{28,24},{1,5},{5... | collective-permute-start | bytes 786440 | tf_op jit(solution)/shard_map/ppermute | solution.py:60
  13.9 9.6 %collective-permute-start.1 = (f32[256,256]{1,0:T(8,128)S(1)}, f32[256,256]{1,0:T(8,128)S(1)}, u32[]{:S(2)}, u32[]{:S(2)}) collective-permute-start(f32[256,256]{1,0:T(8,128)S(1)} %get-tuple-element.118.refs_4_), channel_id=1, source_target_pairs={{0,8},{4,12},{8,16},{12,20},{16,24},{20,28},{24,0},{28,4},{1,9},{5... | collective-permute-start | bytes 786440 | tf_op jit(solution)/shard_map/ppermute | solution.py:129
  23.5 11.0 %collective-permute-start.2 = (f32[2,256,256]{2,1,0:T(8,128)S(1)}, f32[2,256,256]{2,1,0:T(8,128)S(1)}, u32[]{:S(2)}, u32[]{:S(2)}) collective-permute-start(f32[2,256,256]{2,1,0:T(8,128)S(1)} %maximum_bitcast_fusion.refs_0_), channel_id=1, source_target_pairs={{0,1},{1,0},{2,3},{3,2},{4,5},{5,4},{6,7},{7,6},{8,9},{9,8},{10,11... | collective-permute-start | bytes 1572872 | tf_op jit(solution)/shard_map/ppermute | solution.py:63
  23.6 11.0 %collective-permute-start.8 = (f32[256,256]{1,0:T(8,128)S(1)}, f32[256,256]{1,0:T(8,128)S(1)}, u32[]{:S(2)}, u32[]{:S(2)}) collective-permute-start(f32[256,256]{1,0:T(8,128)S(1)} %get-tuple-element.117.refs_4_), channel_id=1, source_target_pairs={{0,8},{4,12},{8,16},{12,20},{16,24},{20,28},{24,0},{28,4},{1,9},{5... | collective-permute-start | bytes 786440 | tf_op jit(solution)/shard_map/ppermute | solution.py:76
  23.7 16.5 %collective-permute-start.13 = (f32[1,256,256]{2,1,0:T(8,128)S(1)}, f32[1,256,256]{2,1,0:T(8,128)S(1)}, u32[]{:S(2)}, u32[]{:S(2)}) collective-permute-start(f32[1,256,256]{2,1,0:T(8,128)S(1)} %get-tuple-element.64), channel_id=1, source_target_pairs={{0,4},{4,0},{8,12},{12,8},{16,20},{20,16},{24,28},{28,24},{1,5},{5... | collective-permute-start | bytes 786440 | tf_op jit(solution)/shard_map/ppermute | solution.py:60
  24.4 15.7 %collective-permute-start.5 = (f32[256,256]{1,0:T(8,128)S(1)}, f32[256,256]{1,0:T(8,128)S(1)}, u32[]{:S(2)}, u32[]{:S(2)}) collective-permute-start(f32[256,256]{1,0:T(8,128)S(1)} %collective-permute-done.1.refs_5_), channel_id=1, source_target_pairs={{0,8},{4,12},{8,16},{12,20},{16,24},{20,28},{24,0},{28,4},{1,9},{5... | collective-permute-start | bytes 786440 | tf_op jit(solution)/shard_map/ppermute | solution.py:76
  34.6 10.8 %collective-permute-start.9 = (f32[256,256]{1,0:T(8,128)S(1)}, f32[256,256]{1,0:T(8,128)S(1)}, u32[]{:S(2)}, u32[]{:S(2)}) collective-permute-start(f32[256,256]{1,0:T(8,128)S(1)} %collective-permute-done.8.refs_5_), channel_id=1, source_target_pairs={{0,8},{4,12},{8,16},{12,20},{16,24},{20,28},{24,0},{28,4},{1,9},{5... | collective-permute-start | bytes 786440 | tf_op jit(solution)/shard_map/ppermute | solution.py:76
  46.3 134.7 %all-gather.7.cloned.1.call-start = ((), (), s32[]{:S(2)}) async-start(), calls=%async_computation | async-start | bytes 7864320 | tf_op jit(solution)/shard_map/all_gather | solution.py:124
  46.3 21.3 %collective-permute-start.3 = (f32[2,256,256]{2,1,0:T(8,128)S(1)}, f32[2,256,256]{2,1,0:T(8,128)S(1)}, u32[]{:S(2)}, u32[]{:S(2)}) collective-permute-start(f32[2,256,256]{2,1,0:T(8,128)S(1)} %maximum_bitcast_fusion.refs_0_), channel_id=1, source_target_pairs={{0,2},{1,3},{2,0},{3,1},{4,6},{5,7},{6,4},{7,5},{8,10},{9,11},{10,... | collective-permute-start | bytes 1572872 | tf_op jit(solution)/shard_map/ppermute | solution.py:63
  67.6 20.0 %collective-permute-start.12 = (f32[3,256,256]{2,1,0:T(8,128)S(1)}, f32[3,256,256]{2,1,0:T(8,128)S(1)}, u32[]{:S(2)}, u32[]{:S(2)}) collective-permute-start(f32[3,256,256]{2,1,0:T(8,128)S(1)} %get-tuple-element.62), channel_id=1, source_target_pairs={{0,4},{4,0},{8,12},{12,8},{16,20},{20,16},{24,28},{28,24},{1,5},{5... | collective-permute-start | bytes 2359304 | tf_op jit(solution)/shard_map/ppermute | solution.py:60
  67.6 11.0 %collective-permute-start.6 = (f32[256,256]{1,0:T(8,128)S(1)}, f32[256,256]{1,0:T(8,128)S(1)}, u32[]{:S(2)}, u32[]{:S(2)}) collective-permute-start(f32[256,256]{1,0:T(8,128)S(1)} %copy-done.26), channel_id=1, source_target_pairs={{0,8},{4,12},{8,16},{12,20},{16,24},{20,28},{24,0},{28,4},{1,9},{5... | collective-permute-start | bytes 786440 | tf_op jit(solution)/shard_map/ppermute | solution.py:76
  69.5 14.2 %collective-permute-start.10 = (f32[256,256]{1,0:T(8,128)S(1)}, f32[256,256]{1,0:T(8,128)S(1)}, u32[]{:S(2)}, u32[]{:S(2)}) collective-permute-start(f32[256,256]{1,0:T(8,128)S(1)} %copy-done.23), channel_id=1, source_target_pairs={{0,8},{4,12},{8,16},{12,20},{16,24},{20,28},{24,0},{28,4},{1,9},{5... | collective-permute-start | bytes 786440 | tf_op jit(solution)/shard_map/ppermute | solution.py:76
  88.8 171.9 %all-gather.11.cloned.1.call-start = ((), (), s32[]{:S(2)}) async-start(), calls=%async_computation.2 | async-start | bytes 13107200 | tf_op jit(solution)/shard_map/all_gather | solution.py:124
  92.9 9.3 %collective-permute-start.7 = (f32[256,256]{1,0:T(8,128)S(1)}, f32[256,256]{1,0:T(8,128)S(1)}, u32[]{:S(2)}, u32[]{:S(2)}) collective-permute-start(f32[256,256]{1,0:T(8,128)S(1)} %get-tuple-element.57), channel_id=1, source_target_pairs={{0,4},{4,0},{8,12},{12,8},{16,20},{20,16},{24,28},{28,24},{1,5},{5... | collective-permute-start | bytes 786440 | tf_op jit(solution)/shard_map/ppermute | solution.py:60
  94.4 12.1 %collective-permute-start.11 = (f32[256,256]{1,0:T(8,128)S(1)}, f32[256,256]{1,0:T(8,128)S(1)}, u32[]{:S(2)}, u32[]{:S(2)}) collective-permute-start(f32[256,256]{1,0:T(8,128)S(1)} %get-tuple-element.61), channel_id=1, source_target_pairs={{0,4},{4,0},{8,12},{12,8},{16,20},{20,16},{24,28},{28,24},{1,5},{5... | collective-permute-start | bytes 786440 | tf_op jit(solution)/shard_map/ppermute | solution.py:60
  106.5 37.5 %collective-permute-start.30 = (f32[5,256,256]{2,1,0:T(8,128)S(1)}, f32[5,256,256]{2,1,0:T(8,128)S(1)}, u32[]{:S(2)}, u32[]{:S(2)}) collective-permute-start(f32[5,256,256]{2,1,0:T(8,128)S(1)} %get-tuple-element.77), channel_id=1, source_target_pairs={{0,4},{4,0},{8,12},{12,8},{16,20},{20,16},{24,28},{28,24},{1,5},{5... | collective-permute-start | bytes 3932168 | tf_op jit(solution)/shard_map/ppermute | solution.py:60
  107.1 11.0 %collective-permute-start.14 = (f32[256,256]{1,0:T(8,128)S(1)}, f32[256,256]{1,0:T(8,128)S(1)}, u32[]{:S(2)}, u32[]{:S(2)}) collective-permute-start(f32[256,256]{1,0:T(8,128)S(1)} %add.56.refs_1_), channel_id=1, source_target_pairs={{0,8},{4,12},{8,16},{12,20},{16,24},{20,28},{24,0},{28,4},{1,9},{5... | collective-permute-start | bytes 786440 | tf_op jit(solution)/shard_map/ppermute | solution.py:76
  107.1 16.7 %collective-permute-start.22 = (f32[256,256]{1,0:T(8,128)S(1)}, f32[256,256]{1,0:T(8,128)S(1)}, u32[]{:S(2)}, u32[]{:S(2)}) collective-permute-start(f32[256,256]{1,0:T(8,128)S(1)} %add.57.refs_1_), channel_id=1, source_target_pairs={{0,8},{4,12},{8,16},{12,20},{16,24},{20,28},{24,0},{28,4},{1,9},{5... | collective-permute-start | bytes 786440 | tf_op jit(solution)/shard_map/ppermute | solution.py:76
  118.1 11.2 %collective-permute-start.15 = (f32[256,256]{1,0:T(8,128)S(1)}, f32[256,256]{1,0:T(8,128)S(1)}, u32[]{:S(2)}, u32[]{:S(2)}) collective-permute-start(f32[256,256]{1,0:T(8,128)S(1)} %collective-permute-done.14.refs_2_), channel_id=1, source_target_pairs={{0,8},{4,12},{8,16},{12,20},{16,24},{20,28},{24,0},{28,4},{1,9},{5... | collective-permute-start | bytes 786440 | tf_op jit(solution)/shard_map/ppermute | solution.py:76
  123.7 11.2 %collective-permute-start.23 = (f32[256,256]{1,0:T(8,128)S(1)}, f32[256,256]{1,0:T(8,128)S(1)}, u32[]{:S(2)}, u32[]{:S(2)}) collective-permute-start(f32[256,256]{1,0:T(8,128)S(1)} %collective-permute-done.22.refs_2_), channel_id=1, source_target_pairs={{0,8},{4,12},{8,16},{12,20},{16,24},{20,28},{24,0},{28,4},{1,9},{5... | collective-permute-start | bytes 786440 | tf_op jit(solution)/shard_map/ppermute | solution.py:76
  129.3 11.2 %collective-permute-start.16 = (f32[256,256]{1,0:T(8,128)S(1)}, f32[256,256]{1,0:T(8,128)S(1)}, u32[]{:S(2)}, u32[]{:S(2)}) collective-permute-start(f32[256,256]{1,0:T(8,128)S(1)} %collective-permute-done.15.refs_3_), channel_id=1, source_target_pairs={{0,8},{4,12},{8,16},{12,20},{16,24},{20,28},{24,0},{28,4},{1,9},{5... | collective-permute-start | bytes 786440 | tf_op jit(solution)/shard_map/ppermute | solution.py:76
  135.0 9.1 %collective-permute-start.24 = (f32[256,256]{1,0:T(8,128)S(1)}, f32[256,256]{1,0:T(8,128)S(1)}, u32[]{:S(2)}, u32[]{:S(2)}) collective-permute-start(f32[256,256]{1,0:T(8,128)S(1)} %collective-permute-done.23.refs_3_), channel_id=1, source_target_pairs={{0,8},{4,12},{8,16},{12,20},{16,24},{20,28},{24,0},{28,4},{1,9},{5... | collective-permute-start | bytes 786440 | tf_op jit(solution)/shard_map/ppermute | solution.py:76
  149.5 9.0 %collective-permute-start.17 = (f32[256,256]{1,0:T(8,128)S(1)}, f32[256,256]{1,0:T(8,128)S(1)}, u32[]{:S(2)}, u32[]{:S(2)}) collective-permute-start(f32[256,256]{1,0:T(8,128)S(1)} %get-tuple-element.67), channel_id=1, source_target_pairs={{0,4},{4,0},{8,12},{12,8},{16,20},{20,16},{24,28},{28,24},{1,5},{5... | collective-permute-start | bytes 786440 | tf_op jit(solution)/shard_map/ppermute | solution.py:60
  152.0 9.4 %collective-permute-start.25 = (f32[256,256]{1,0:T(8,128)S(1)}, f32[256,256]{1,0:T(8,128)S(1)}, u32[]{:S(2)}, u32[]{:S(2)}) collective-permute-start(f32[256,256]{1,0:T(8,128)S(1)} %get-tuple-element.71), channel_id=1, source_target_pairs={{0,4},{4,0},{8,12},{12,8},{16,20},{20,16},{24,28},{28,24},{1,5},{5... | collective-permute-start | bytes 786440 | tf_op jit(solution)/shard_map/ppermute | solution.py:60
  158.6 11.0 %collective-permute-start.18 = (f32[256,256]{1,0:T(8,128)S(1)}, f32[256,256]{1,0:T(8,128)S(1)}, u32[]{:S(2)}, u32[]{:S(2)}) collective-permute-start(f32[256,256]{1,0:T(8,128)S(1)} %add.58.refs_1_), channel_id=1, source_target_pairs={{0,8},{4,12},{8,16},{12,20},{16,24},{20,28},{24,0},{28,4},{1,9},{5... | collective-permute-start | bytes 786440 | tf_op jit(solution)/shard_map/ppermute | solution.py:76
  161.4 13.9 %collective-permute-start.26 = (f32[256,256]{1,0:T(8,128)S(1)}, f32[256,256]{1,0:T(8,128)}, u32[]{:S(2)}, u32[]{:S(2)}) collective-permute-start(f32[256,256]{1,0:T(8,128)S(1)} %add.60.refs_1_), channel_id=1, source_target_pairs={{0,8},{4,12},{8,16},{12,20},{16,24},{20,28},{24,0},{28,4},{1,9},{5... | collective-permute-start | bytes 786440 | tf_op jit(solution)/shard_map/ppermute | solution.py:76
  169.6 11.3 %collective-permute-start.19 = (f32[256,256]{1,0:T(8,128)S(1)}, f32[256,256]{1,0:T(8,128)}, u32[]{:S(2)}, u32[]{:S(2)}) collective-permute-start(f32[256,256]{1,0:T(8,128)S(1)} %collective-permute-done.18.refs_2_), channel_id=1, source_target_pairs={{0,8},{4,12},{8,16},{12,20},{16,24},{20,28},{24,0},{28,4},{1,9},{5... | collective-permute-start | bytes 786440 | tf_op jit(solution)/shard_map/ppermute | solution.py:76
  175.3 11.5 %collective-permute-start.27 = (f32[256,256]{1,0:T(8,128)}, f32[256,256]{1,0:T(8,128)}, u32[]{:S(2)}, u32[]{:S(2)}) collective-permute-start(f32[256,256]{1,0:T(8,128)} %collective-permute-done.26.refs_2_), channel_id=1, source_target_pairs={{0,8},{4,12},{8,16},{12,20},{16,24},{20,28},{24,0},{28,4},{1,9},{5... | collective-permute-start | bytes 786440 | tf_op jit(solution)/shard_map/ppermute | solution.py:76
  180.9 10.2 %collective-permute-start.20 = (f32[256,256]{1,0:T(8,128)}, f32[256,256]{1,0:T(8,128)}, u32[]{:S(2)}, u32[]{:S(2)}) collective-permute-start(f32[256,256]{1,0:T(8,128)} %collective-permute-done.19.refs_3_), channel_id=1, source_target_pairs={{0,8},{4,12},{8,16},{12,20},{16,24},{20,28},{24,0},{28,4},{1,9},{5... | collective-permute-start | bytes 786440 | tf_op jit(solution)/shard_map/ppermute | solution.py:76
  200.7 11.1 %collective-permute-start.31 = (f32[256,256]{1,0:T(8,128)S(1)}, f32[256,256]{1,0:T(8,128)S(1)}, u32[]{:S(2)}, u32[]{:S(2)}) collective-permute-start(f32[256,256]{1,0:T(8,128)S(1)} %add.59.refs_1_), channel_id=1, source_target_pairs={{0,8},{4,12},{8,16},{12,20},{16,24},{20,28},{24,0},{28,4},{1,9},{5... | collective-permute-start | bytes 786440 | tf_op jit(solution)/shard_map/ppermute | solution.py:76
  204.2 13.3 %collective-permute-start.39 = (f32[256,256]{1,0:T(8,128)S(1)}, f32[256,256]{1,0:T(8,128)S(1)}, u32[]{:S(2)}, u32[]{:S(2)}) collective-permute-start(f32[256,256]{1,0:T(8,128)S(1)} %add.61.refs_1_), channel_id=1, source_target_pairs={{0,8},{4,12},{8,16},{12,20},{16,24},{20,28},{24,0},{28,4},{1,9},{5... | collective-permute-start | bytes 786440 | tf_op jit(solution)/shard_map/ppermute | solution.py:76
  211.8 11.2 %collective-permute-start.32 = (f32[256,256]{1,0:T(8,128)S(1)}, f32[256,256]{1,0:T(8,128)S(1)}, u32[]{:S(2)}, u32[]{:S(2)}) collective-permute-start(f32[256,256]{1,0:T(8,128)S(1)} %collective-permute-done.31.refs_2_), channel_id=1, source_target_pairs={{0,8},{4,12},{8,16},{12,20},{16,24},{20,28},{24,0},{28,4},{1,9},{5... | collective-permute-start | bytes 786440 | tf_op jit(solution)/shard_map/ppermute | solution.py:76
  217.4 11.2 %collective-permute-start.40 = (f32[256,256]{1,0:T(8,128)S(1)}, f32[256,256]{1,0:T(8,128)S(1)}, u32[]{:S(2)}, u32[]{:S(2)}) collective-permute-start(f32[256,256]{1,0:T(8,128)S(1)} %collective-permute-done.39.refs_2_), channel_id=1, source_target_pairs={{0,8},{4,12},{8,16},{12,20},{16,24},{20,28},{24,0},{28,4},{1,9},{5... | collective-permute-start | bytes 786440 | tf_op jit(solution)/shard_map/ppermute | solution.py:76
  228.6 10.6 %collective-permute-start.41 = (f32[256,256]{1,0:T(8,128)S(1)}, f32[256,256]{1,0:T(8,128)S(1)}, u32[]{:S(2)}, u32[]{:S(2)}) collective-permute-start(f32[256,256]{1,0:T(8,128)S(1)} %collective-permute-done.40.refs_3_), channel_id=1, source_target_pairs={{0,8},{4,12},{8,16},{12,20},{16,24},{20,28},{24,0},{28,4},{1,9},{5... | collective-permute-start | bytes 786440 | tf_op jit(solution)/shard_map/ppermute | solution.py:76
  240.5 11.0 %collective-permute-start.35 = (f32[256,256]{1,0:T(8,128)S(1)}, f32[256,256]{1,0:T(8,128)S(1)}, u32[]{:S(2)}, u32[]{:S(2)}) collective-permute-start(f32[256,256]{1,0:T(8,128)S(1)} %add.62.refs_1_), channel_id=1, source_target_pairs={{0,8},{4,12},{8,16},{12,20},{16,24},{20,28},{24,0},{28,4},{1,9},{5... | collective-permute-start | bytes 786440 | tf_op jit(solution)/shard_map/ppermute | solution.py:76
  246.9 11.1 %collective-permute-start.43 = (f32[256,256]{1,0:T(8,128)S(1)}, f32[256,256]{1,0:T(8,128)}, u32[]{:S(2)}, u32[]{:S(2)}) collective-permute-start(f32[256,256]{1,0:T(8,128)S(1)} %add.64.refs_1_), channel_id=1, source_target_pairs={{0,8},{4,12},{8,16},{12,20},{16,24},{20,28},{24,0},{28,4},{1,9},{5... | collective-permute-start | bytes 786440 | tf_op jit(solution)/shard_map/ppermute | solution.py:76
  251.5 9.2 %collective-permute-start.36 = (f32[256,256]{1,0:T(8,128)S(1)}, f32[256,256]{1,0:T(8,128)}, u32[]{:S(2)}, u32[]{:S(2)}) collective-permute-start(f32[256,256]{1,0:T(8,128)S(1)} %collective-permute-done.35.refs_2_), channel_id=1, source_target_pairs={{0,8},{4,12},{8,16},{12,20},{16,24},{20,28},{24,0},{28,4},{1,9},{5... | collective-permute-start | bytes 786440 | tf_op jit(solution)/shard_map/ppermute | solution.py:76
  257.9 12.2 %collective-permute-start.44 = (f32[256,256]{1,0:T(8,128)}, f32[256,256]{1,0:T(8,128)}, u32[]{:S(2)}, u32[]{:S(2)}) collective-permute-start(f32[256,256]{1,0:T(8,128)} %collective-permute-done.43.refs_2_), channel_id=1, source_target_pairs={{0,8},{4,12},{8,16},{12,20},{16,24},{20,28},{24,0},{28,4},{1,9},{5... | collective-permute-start | bytes 786440 | tf_op jit(solution)/shard_map/ppermute | solution.py:76
  260.8 9.7 %collective-permute-start.37 = (f32[256,256]{1,0:T(8,128)}, f32[256,256]{1,0:T(8,128)}, u32[]{:S(2)}, u32[]{:S(2)}) collective-permute-start(f32[256,256]{1,0:T(8,128)} %collective-permute-done.36.refs_3_), channel_id=1, source_target_pairs={{0,8},{4,12},{8,16},{12,20},{16,24},{20,28},{24,0},{28,4},{1,9},{5... | collective-permute-start | bytes 786440 | tf_op jit(solution)/shard_map/ppermute | solution.py:76
  270.1 10.0 %collective-permute-start.45 = (f32[256,256]{1,0:T(8,128)}, f32[256,256]{1,0:T(8,128)S(1)}, u32[]{:S(2)}, u32[]{:S(2)}) collective-permute-start(f32[256,256]{1,0:T(8,128)} %collective-permute-done.44.refs_3_), channel_id=1, source_target_pairs={{0,8},{4,12},{8,16},{12,20},{16,24},{20,28},{24,0},{28,4},{1,9},{5... | collective-permute-start | bytes 786440 | tf_op jit(solution)/shard_map/ppermute | solution.py:76
  272.7 12.3 %collective-permute-start.38 = (f32[256,256]{1,0:T(8,128)S(1)}, f32[256,256]{1,0:T(8,128)S(1)}, u32[]{:S(2)}, u32[]{:S(2)}) collective-permute-start(f32[256,256]{1,0:T(8,128)S(1)} %get-tuple-element.83), channel_id=1, source_target_pairs={{0,4},{4,0},{8,12},{12,8},{16,20},{20,16},{24,28},{28,24},{1,5},{5... | collective-permute-start | bytes 786440 | tf_op jit(solution)/shard_map/ppermute | solution.py:60
  285.1 10.5 %collective-permute-start.47 = (f32[256,256]{1,0:T(8,128)S(1)}, f32[256,256]{1,0:T(8,128)S(1)}, u32[]{:S(2)}, u32[]{:S(2)}) collective-permute-start(f32[256,256]{1,0:T(8,128)S(1)} %add.63.refs_1_), channel_id=1, source_target_pairs={{0,8},{4,12},{8,16},{12,20},{16,24},{20,28},{24,0},{28,4},{1,9},{5... | collective-permute-start | bytes 786440 | tf_op jit(solution)/shard_map/ppermute | solution.py:76
  289.4 10.5 %collective-permute-start.55 = (f32[256,256]{1,0:T(8,128)S(1)}, f32[256,256]{1,0:T(8,128)S(1)}, u32[]{:S(2)}, u32[]{:S(2)}) collective-permute-start(f32[256,256]{1,0:T(8,128)S(1)} %add.65.refs_1_), channel_id=1, source_target_pairs={{0,8},{4,12},{8,16},{12,20},{16,24},{20,28},{24,0},{28,4},{1,9},{5... | collective-permute-start | bytes 786440 | tf_op jit(solution)/shard_map/ppermute | solution.py:76
  299.9 10.8 %collective-permute-start.56 = (f32[256,256]{1,0:T(8,128)S(1)}, f32[256,256]{1,0:T(8,128)S(1)}, u32[]{:S(2)}, u32[]{:S(2)}) collective-permute-start(f32[256,256]{1,0:T(8,128)S(1)} %collective-permute-done.55.refs_2_), channel_id=1, source_target_pairs={{0,8},{4,12},{8,16},{12,20},{16,24},{20,28},{24,0},{28,4},{1,9},{5... | collective-permute-start | bytes 786440 | tf_op jit(solution)/shard_map/ppermute | solution.py:76
  303.8 12.5 %collective-permute-start.49 = (f32[256,256]{1,0:T(8,128)S(1)}, f32[256,256]{1,0:T(8,128)S(1)}, u32[]{:S(2)}, u32[]{:S(2)}) collective-permute-start(f32[256,256]{1,0:T(8,128)S(1)} %collective-permute-done.48.refs_3_), channel_id=1, source_target_pairs={{0,8},{4,12},{8,16},{12,20},{16,24},{20,28},{24,0},{28,4},{1,9},{5... | collective-permute-start | bytes 786440 | tf_op jit(solution)/shard_map/ppermute | solution.py:76
  310.7 11.2 %collective-permute-start.57 = (f32[256,256]{1,0:T(8,128)S(1)}, f32[256,256]{1,0:T(8,128)S(1)}, u32[]{:S(2)}, u32[]{:S(2)}) collective-permute-start(f32[256,256]{1,0:T(8,128)S(1)} %collective-permute-done.56.refs_3_), channel_id=1, source_target_pairs={{0,8},{4,12},{8,16},{12,20},{16,24},{20,28},{24,0},{28,4},{1,9},{5... | collective-permute-start | bytes 786440 | tf_op jit(solution)/shard_map/ppermute | solution.py:76
  324.7 10.2 %collective-permute-start.51 = (f32[256,256]{1,0:T(8,128)S(1)}, f32[256,256]{1,0:T(8,128)S(1)}, u32[]{:S(2)}, u32[]{:S(2)}) collective-permute-start(f32[256,256]{1,0:T(8,128)S(1)} %add.66.refs_1_), channel_id=1, source_target_pairs={{0,8},{4,12},{8,16},{12,20},{16,24},{20,28},{24,0},{28,4},{1,9},{5... | collective-permute-start | bytes 786440 | tf_op jit(solution)/shard_map/ppermute | solution.py:76
  (64 other events, 386.5 us)
Sparse Core Ops, SparseCore 0:
  46.4 26.2 all-gather.8
  88.9 44.6 all-gather.6
  146.0 69.1 all-gather.10
where the time goes:
time: 383 us; the launch traced here: 382 us
  waiting for transfers between devices  282 us (74%)
  starting transfers between devices  29.3 us (8%)
  Pallas kernels  27 us (7%)
  local copies, waits for them, and re-layouts  21.1 us (6%)
  between operations  14.6 us (4%)
  other arithmetic  8.53 us (2%)
    ppermute x41, waiting for transfers between devices, ring_of(): slots[i].append(lax.ppermute(value, 'row', ring))  197 us
    ppermute x18, waiting for transfers between devices, swap(): return lax.ppermute(value, 'row', pair)  48.6 us
    pallas_call x20, Pallas kernels, product(): pl.pallas_call(functools.partial(product_kernel, layers, sign, len(pieces...  27 us
    ppermute x18, starting transfers between devices, swap(): return lax.ppermute(value, 'row', pair)  21.8 us
    ppermute x3, waiting for transfers between devices, cross(): return lax.ppermute(value, 'col', [(c, c ^ bits) for c in range(cols)])  19.8 us
    ppermute x3, waiting for transfers between devices, body(): lax.ppermute(totals, 'row', [(r, r ^ bit) for r in range(rows)])  10 us
    all_gather x2, local copies, waits for them, and re-layouts, fetch(): whole = lax.all_gather(piece, 'col', axis=0)  8.27 us
  transfers between devices with their start and end apart: 69, of which 57 were waited for; matrix products, arithmetic and copies ran while one was open for 4% of the time, Pallas kernels for 7%

commit v1 on v0

--- a/solution.py
+++ b/solution.py
@@ -30,7 +30,7 @@
         xh[pl.ds(start, height), :], xl[pl.ds(start, height), :] = halves(ref[...])
     for half, out in ((1, away), (0, own)):
         for slot in range(layers):
-            block = factor[slot][half] if pieces > 1 else factor[0][slot, 0, half]
+            block = factor[slot][half] if pieces > 1 else factor[0][slot, half, 0]
             section = slice(slot * height, (slot + 1) * height)
             fh[:, section], fl[:, section] = halves(block)
         total = dot(fl[...], xh[...]) + dot(fh[...], xl[...]) + dot(fh[...], xh[...])
@@ -47,6 +47,8 @@
     pair = [(r, r ^ 1) for r in range(rows)]
 
     ring = [(r, (r + 2) % rows) for r in range(rows)]
+    climb = [[(r, r + 2) for r in range(2 * hop, rows - 2)] for hop in range(layers - 1)]
+    circle = [ring] * (layers - 1)
 
     def body(lower, dinv, kcols, prior):
         segments, height, breadth = kcols.shape
@@ -66,14 +68,14 @@
             even, odd = blocks[..., :height], blocks[..., height:]
             return jnp.where(parity == 0, even, odd), jnp.where(parity == 0, odd, even)
 
-        def ring_of(panels, waits={}):
+        def ring_of(panels, route, waits={}):
             slots = [[panel] for panel in panels]
             for hop in range(1, layers):
                 for i in range(streams):
                     value = slots[i][-1]
                     if (i, hop) in waits:
                         value = after(value, *waits[i, hop])
-                    slots[i].append(lax.ppermute(value, "row", ring))
+                    slots[i].append(lax.ppermute(value, "row", route[hop - 1]))
             return slots, [[stream[hop] for stream in slots] for hop in range(layers)]
 
         def block_spec(shape):
@@ -84,7 +86,7 @@
                 pieces, specs = factor, [block_spec(piece.shape) for piece in factor]
             else:
                 pieces, index = [factor[0]], factor[1]
-                specs = [pl.BlockSpec((cols, 1, 2, height, height), lambda i: (0, index, 0, 0, 0))]
+                specs = [pl.BlockSpec((cols, 2, 1, height, height), lambda i: (0, 0, index, 0, 0))]
             wide = panels[0].shape[1]
             depth = layers * height
             shape = jax.ShapeDtypeStruct((height, wide), jnp.float32)
@@ -115,7 +117,7 @@
         def exchange(keys, start, use):
             mine, theirs = by_parity(jnp.stack([block(s, t) for s, t in keys]))
             got = swap(after(theirs, *start) if start else theirs)
-            return jnp.stack([mine, after(got, *use)], axis=-3), got
+            return jnp.stack([mine, after(got, *use)]), got
 
         found = {}
 
@@ -126,24 +128,19 @@
                 found[key] = (whole, index)
 
         firsts = [kcols[0, :, c] for c in cut]
-        one = lax.ppermute(firsts[0], "row", ring)
-        piece, got = exchange([(0, 0)], [], [one])
-        near = cross(piece[0], 1)
-        beside = cross(piece[0], 2)
-        far = cross(after(beside, near), 1)
-        found[0, 0] = [piece[0], near, beside, far]
-        slots, hops = ring_of(firsts, {(streams - 1, 2): [near], (streams - 1, 3): [far]})
-        fetch([(1, 0)], [got], hops[2])
-        fetch([(1, 1), (2, 0), (2, 1)], [got, *hops[2]], hops[3])
+        slots, hops = ring_of(firsts, climb)
+        fetch([(0, 0)], [], hops[1][:1])
+        fetch([(1, 0)], hops[1], hops[2])
+        fetch([(1, 1)], hops[2][:1], hops[3])
         for s in range(segments):
             for i in range(streams):
                 own, away = product(found[s, s], slots[i])
                 solved[i][s] = own + swap(away)
             if s + 1 == segments:
                 break
-            panels, after_x = ring_of([solved[i][s] for i in range(streams)])
+            panels, after_x = ring_of([solved[i][s] for i in range(streams)], circle)
             if s == 0:
-                fetch([(2, 2), (3, 0), (3, 1), (3, 2), (3, 3)], after_x[0], after_x[3])
+                fetch([(2, 0), (2, 1), (2, 2)], after_x[0], after_x[2])
             residuals = []
             for i in range(streams):
                 own, away = product(found[s + 1, s], panels[i], sums[i][s + 1], -1)
@@ -159,7 +156,9 @@
                     sums[i][3] = product(found[3, 1], panels[i], sums[i][3], -1)
                     early.append(sums[i][3][0])
             first_panels = panels
-            slots, hops = ring_of(residuals, {(streams - 1, 3): early} if early else {})
+            slots, hops = ring_of(residuals, climb)
+            if s == 0:
+                fetch([(3, 0), (3, 1), (3, 2), (3, 3)], hops[0], hops[2])
         solution = jnp.stack(
             [jnp.concatenate([solved[i][s] for i in range(streams)], axis=1) for s in range(segments)]
         )

time: 383 us -> 348 us (0.909)
  waiting for transfers between devices: 282 us -> 152 us
  starting transfers between devices: 29.3 us -> 119 us
  Pallas kernels: 27 us -> 30.9 us
    ppermute x45 -> x42, waiting for transfers between devices: 223 us -> 87.6 us  [ring_of(): slots[i].append(lax.ppermute(value, 'row', route[hop - 1]))]
    ppermute x45 -> x42, starting transfers between devices: 5.76 us -> 75 us  [ring_of(): slots[i].append(lax.ppermute(value, 'row', route[hop - 1]))]
    ppermute x3, starting transfers between devices: 1.62 us -> 20.5 us  [body(): lax.ppermute(totals, 'row', [(r, r ^ bit) for r in range(rows)])]
    ppermute x18 -> x19, waiting for transfers between devices: 48.6 us -> 59.5 us  [swap(): return lax.ppermute(value, 'row', pair)]
    unnamed x82 -> x60, local copies, waits for them, and re-layouts: 7.32 us -> 17 us
    all_gather x2 -> x0, local copies, waits for them, and re-layouts: 8.27 us -> none  [fetch(): whole = lax.all_gather(piece, 'col', axis=0)]
    ppermute x3, waiting for transfers between devices: 10 us -> 5.05 us  [body(): lax.ppermute(totals, 'row', [(r, r ^ bit) for r in range(rows)])]
    pallas_call x20, Pallas kernels: 27 us -> 30.9 us  [product(): pl.pallas_call(functools.partial(product_kernel, layers, sign, len(pieces...]
  transfers between devices with their start and end apart: 69 -> 69, of which waited for: 57 -> 39; matrix products, arithmetic and copies ran while one was open for 4% -> 2% of each run, Pallas kernels for 7% -> 9%
where the time goes in v1:
time: 348 us; the launch traced here: 346 us
  waiting for transfers between devices  152 us (44%)
  starting transfers between devices  119 us (34%)
  Pallas kernels  30.9 us (9%)
  local copies, waits for them, and re-layouts  18.7 us (5%)
  between operations  14.6 us (4%)
  other arithmetic  10.9 us (3%)
    ppermute x42, waiting for transfers between devices, ring_of(): slots[i].append(lax.ppermute(value, 'row', route[hop - 1]))  87.6 us
    ppermute x42, starting transfers between devices, ring_of(): slots[i].append(lax.ppermute(value, 'row', route[hop - 1]))  75 us
    ppermute x19, waiting for transfers between devices, swap(): return lax.ppermute(value, 'row', pair)  59.5 us
    pallas_call x20, Pallas kernels, product(): pl.pallas_call(functools.partial(product_kernel, layers, sign, len(pieces...  30.9 us
    ppermute x19, starting transfers between devices, swap(): return lax.ppermute(value, 'row', pair)  23.4 us
    ppermute x3, starting transfers between devices, body(): lax.ppermute(totals, 'row', [(r, r ^ bit) for r in range(rows)])  20.5 us
    unnamed x60, local copies, waits for them, and re-layouts  17 us
    another operation x9, other arithmetic, exchange(): return (jnp.stack([mine, after(got, *use)]), got)  8.1 us
  transfers between devices with their start and end apart: 69, of which 39 were waited for; matrix products, arithmetic and copies ran while one was open for 2% of the time, Pallas kernels for 9%

profile of v1, /device:TPU:0, one launch (start us, length us, event | category | flops | bytes accessed | tf_op | source)
XLA Modules:
  0.0 346.4 jit_solution(10658286755218799557)
XLA Ops:
  8.7 3.0 collective-permute-start
  12.7 3.5 %collective-permute-start.1 = (f32[256,256]{1,0:T(8,128)S(1)}, f32[256,256]{1,0:T(8,128)S(1)}, u32[]{:S(2)}, u32[]{:S(2)}) collective-permute-start(f32[256,256]{1,0:T(8,128)S(1)} %get-tuple-element.110.refs_1_), channel_id=1, source_target_pairs={{0,8},{4,12},{8,16},{12,20},{16,24},{20,28},{1,9},{5,13},{9,17},{1... | collective-permute-start | bytes 786440 | tf_op jit(solution)/shard_map/ppermute | solution.py:78
  18.0 3.4 collective-permute-done.1.refs_2_
  22.3 4.4 %collective-permute-start.5 = (f32[256,256]{1,0:T(8,128)S(1)}, f32[256,256]{1,0:T(8,128)S(1)}, u32[]{:S(2)}, u32[]{:S(2)}) collective-permute-start(f32[256,256]{1,0:T(8,128)S(1)} %get-tuple-element.109.refs_1_), channel_id=1, source_target_pairs={{0,8},{4,12},{8,16},{12,20},{16,24},{20,28},{1,9},{5,13},{9,17},{1... | collective-permute-start | bytes 786440 | tf_op jit(solution)/shard_map/ppermute | solution.py:78
  27.8 3.3 collective-permute-done.5.refs_2_
  33.3 4.9 %collective-permute-done.10 = f32[1,256,256]{2,1,0:T(8,128)S(1)} collective-permute-done((f32[1,256,256]{2,1,0:T(8,128)S(1)}, f32[1,256,256]{2,1,0:T(8,128)S(1)}, u32[]{:S(2)}, u32[]{:S(2)}) %collective-permute-start.10) | collective-permute-done | bytes 262176 | tf_op jit(solution)/shard_map/ppermute | solution.py:62
  41.4 4.9 %collective-permute-done.9 = f32[1,256,256]{2,1,0:T(8,128)S(1)} collective-permute-done((f32[1,256,256]{2,1,0:T(8,128)S(1)}, f32[1,256,256]{2,1,0:T(8,128)S(1)}, u32[]{:S(2)}, u32[]{:S(2)}) %collective-permute-start.9) | collective-permute-done | bytes 262176 | tf_op jit(solution)/shard_map/ppermute | solution.py:62
  53.3 5.8 %collective-permute-done.4 = f32[256,256]{1,0:T(8,128)S(1)} collective-permute-done((f32[256,256]{1,0:T(8,128)S(1)}, f32[256,256]{1,0:T(8,128)S(1)}, u32[]{:S(2)}, u32[]{:S(2)}) %collective-permute-start.4) | collective-permute-done | bytes 262176 | tf_op jit(solution)/shard_map/ppermute | solution.py:62
  59.2 4.0 %collective-permute-done.8 = f32[256,256]{1,0:T(8,128)S(1)} collective-permute-done((f32[256,256]{1,0:T(8,128)S(1)}, f32[256,256]{1,0:T(8,128)S(1)}, u32[]{:S(2)}, u32[]{:S(2)}) %collective-permute-start.8) | collective-permute-done | bytes 262176 | tf_op jit(solution)/shard_map/ppermute | solution.py:62
  64.8 6.4 %collective-permute-start.11 = (f32[256,256]{1,0:T(8,128)S(1)}, f32[256,256]{1,0:T(8,128)S(1)}, u32[]{:S(2)}, u32[]{:S(2)}) collective-permute-start(f32[256,256]{1,0:T(8,128)S(1)} %add.56.refs_1_), channel_id=1, source_target_pairs={{0,8},{4,12},{8,16},{12,20},{16,24},{20,28},{24,0},{28,4},{1,9},{5... | collective-permute-start | bytes 786440 | tf_op jit(solution)/shard_map/ppermute | solution.py:78
  71.1 6.9 %collective-permute-start.19 = (f32[256,256]{1,0:T(8,128)S(1)}, f32[256,256]{1,0:T(8,128)S(1)}, u32[]{:S(2)}, u32[]{:S(2)}) collective-permute-start(f32[256,256]{1,0:T(8,128)S(1)} %add.57.refs_1_), channel_id=1, source_target_pairs={{0,8},{4,12},{8,16},{12,20},{16,24},{20,28},{24,0},{28,4},{1,9},{5... | collective-permute-start | bytes 786440 | tf_op jit(solution)/shard_map/ppermute | solution.py:78
  78.1 8.4 %collective-permute-done.11.refs_2_ = f32[256,256]{1,0:T(8,128)S(1)} collective-permute-done((f32[256,256]{1,0:T(8,128)S(1)}, f32[256,256]{1,0:T(8,128)S(1)}, u32[]{:S(2)}, u32[]{:S(2)}) %collective-permute-start.11) | collective-permute-done | bytes 262176 | tf_op jit(solution)/shard_map/ppermute | solution.py:78
  86.5 5.6 %collective-permute-done.19.refs_2_ = f32[256,256]{1,0:T(8,128)S(1)} collective-permute-done((f32[256,256]{1,0:T(8,128)S(1)}, f32[256,256]{1,0:T(8,128)S(1)}, u32[]{:S(2)}, u32[]{:S(2)}) %collective-permute-start.19) | collective-permute-done | bytes 262176 | tf_op jit(solution)/shard_map/ppermute | solution.py:78
  92.1 2.9 collective-permute-done.12.refs_3_
  95.0 7.3 %collective-permute-done.20.refs_3_ = f32[256,256]{1,0:T(8,128)S(1)} collective-permute-done((f32[256,256]{1,0:T(8,128)S(1)}, f32[256,256]{1,0:T(8,128)S(1)}, u32[]{:S(2)}, u32[]{:S(2)}) %collective-permute-start.20) | collective-permute-done | bytes 262176 | tf_op jit(solution)/shard_map/ppermute | solution.py:78
  103.8 8.1 %collective-permute-done.13.refs_4_ = f32[256,256]{1,0:T(8,128)S(1)} collective-permute-done((f32[256,256]{1,0:T(8,128)S(1)}, f32[256,256]{1,0:T(8,128)S(1)}, u32[]{:S(2)}, u32[]{:S(2)}) %collective-permute-start.13) | collective-permute-done | bytes 262176 | tf_op jit(solution)/shard_map/ppermute | solution.py:78
  118.9 5.1 %collective-permute-done.14 = f32[256,256]{1,0:T(8,128)S(1)} collective-permute-done((f32[256,256]{1,0:T(8,128)S(1)}, f32[256,256]{1,0:T(8,128)S(1)}, u32[]{:S(2)}, u32[]{:S(2)}) %collective-permute-start.14) | collective-permute-done | bytes 262176 | tf_op jit(solution)/shard_map/ppermute | solution.py:62
  124.1 5.6 %collective-permute-done.22 = f32[256,256]{1,0:T(8,128)S(1)} collective-permute-done((f32[256,256]{1,0:T(8,128)S(1)}, f32[256,256]{1,0:T(8,128)S(1)}, u32[]{:S(2)}, u32[]{:S(2)}) %collective-permute-start.22) | collective-permute-done | bytes 262176 | tf_op jit(solution)/shard_map/ppermute | solution.py:62
  133.7 2.5 collective-permute-done.15.refs_2_
  140.5 4.3 %collective-permute-done.44 = f32[4,256,256]{2,1,0:T(8,128)S(1)} collective-permute-done((f32[4,256,256]{2,1,0:T(8,128)S(1)}, f32[4,256,256]{2,1,0:T(8,128)S(1)}, u32[]{:S(2)}, u32[]{:S(2)}) %collective-permute-start.44) | collective-permute-done | bytes 1048608 | tf_op jit(solution)/shard_map/ppermute | solution.py:62
  160.2 3.7 %collective-permute-start.28 = (f32[256,256]{1,0:T(8,128)S(1)}, f32[256,256]{1,0:T(8,128)S(1)}, u32[]{:S(2)}, u32[]{:S(2)}) collective-permute-start(f32[256,256]{1,0:T(8,128)S(1)} %add.59.refs_1_), channel_id=1, source_target_pairs={{0,8},{4,12},{8,16},{12,20},{16,24},{20,28},{24,0},{28,4},{1,9},{5... | collective-permute-start | bytes 786440 | tf_op jit(solution)/shard_map/ppermute | solution.py:78
  163.9 12.9 %collective-permute-start.36 = (f32[256,256]{1,0:T(8,128)S(1)}, f32[256,256]{1,0:T(8,128)S(1)}, u32[]{:S(2)}, u32[]{:S(2)}) collective-permute-start(f32[256,256]{1,0:T(8,128)S(1)} %add.61.refs_1_), channel_id=1, source_target_pairs={{0,8},{4,12},{8,16},{12,20},{16,24},{20,28},{24,0},{28,4},{1,9},{5... | collective-permute-start | bytes 786440 | tf_op jit(solution)/shard_map/ppermute | solution.py:78
  176.8 5.5 %collective-permute-done.28.refs_2_ = f32[256,256]{1,0:T(8,128)S(1)} collective-permute-done((f32[256,256]{1,0:T(8,128)S(1)}, f32[256,256]{1,0:T(8,128)S(1)}, u32[]{:S(2)}, u32[]{:S(2)}) %collective-permute-start.28) | collective-permute-done | bytes 262176 | tf_op jit(solution)/shard_map/ppermute | solution.py:78
  183.1 2.6 collective-permute-done.36.refs_2_
  185.7 4.9 %collective-permute-done.29.refs_3_ = f32[256,256]{1,0:T(8,128)} collective-permute-done((f32[256,256]{1,0:T(8,128)S(1)}, f32[256,256]{1,0:T(8,128)}, u32[]{:S(2)}, u32[]{:S(2)}) %collective-permute-start.29) | collective-permute-done | bytes 262176 | tf_op jit(solution)/shard_map/ppermute | solution.py:78
  190.6 3.2 collective-permute-done.37.refs_3_
  193.9 2.9 copy-done.1
  199.1 2.4 shard_map.66
  207.0 3.7 %collective-permute-done.31 = f32[256,256]{1,0:T(8,128)S(1)} collective-permute-done((f32[256,256]{1,0:T(8,128)S(1)}, f32[256,256]{1,0:T(8,128)S(1)}, u32[]{:S(2)}, u32[]{:S(2)}) %collective-permute-start.31) | collective-permute-done | bytes 262176 | tf_op jit(solution)/shard_map/ppermute | solution.py:62
  212.1 3.5 %collective-permute-done.39 = f32[256,256]{1,0:T(8,128)S(1)} collective-permute-done((f32[256,256]{1,0:T(8,128)S(1)}, f32[256,256]{1,0:T(8,128)S(1)}, u32[]{:S(2)}, u32[]{:S(2)}) %collective-permute-start.39) | collective-permute-done | bytes 262176 | tf_op jit(solution)/shard_map/ppermute | solution.py:62
  217.6 6.0 %collective-permute-done.40.refs_2_ = f32[256,256]{1,0:T(8,128)S(1)} collective-permute-done((f32[256,256]{1,0:T(8,128)S(1)}, f32[256,256]{1,0:T(8,128)S(1)}, u32[]{:S(2)}, u32[]{:S(2)}) %collective-permute-start.40) | collective-permute-done | bytes 262176 | tf_op jit(solution)/shard_map/ppermute | solution.py:78
  229.9 3.2 collective-permute-done.35
  233.2 9.2 %collective-permute-start.45 = (f32[256,256]{1,0:T(8,128)S(1)}, f32[256,256]{1,0:T(8,128)S(1)}, u32[]{:S(2)}, u32[]{:S(2)}) collective-permute-start(f32[256,256]{1,0:T(8,128)S(1)} %add.63.refs_1_), channel_id=1, source_target_pairs={{0,8},{4,12},{8,16},{12,20},{16,24},{20,28},{24,0},{28,4},{1,9},{5... | collective-permute-start | bytes 786440 | tf_op jit(solution)/shard_map/ppermute | solution.py:78
  242.4 7.2 %collective-permute-start.53 = (f32[256,256]{1,0:T(8,128)S(1)}, f32[256,256]{1,0:T(8,128)S(1)}, u32[]{:S(2)}, u32[]{:S(2)}) collective-permute-start(f32[256,256]{1,0:T(8,128)S(1)} %add.65.refs_1_), channel_id=1, source_target_pairs={{0,8},{4,12},{8,16},{12,20},{16,24},{20,28},{24,0},{28,4},{1,9},{5... | collective-permute-start | bytes 786440 | tf_op jit(solution)/shard_map/ppermute | solution.py:78
  249.6 5.6 %collective-permute-done.45.refs_2_ = f32[256,256]{1,0:T(8,128)S(1)} collective-permute-done((f32[256,256]{1,0:T(8,128)S(1)}, f32[256,256]{1,0:T(8,128)S(1)}, u32[]{:S(2)}, u32[]{:S(2)}) %collective-permute-start.45) | collective-permute-done | bytes 262176 | tf_op jit(solution)/shard_map/ppermute | solution.py:78
  255.9 4.9 %collective-permute-done.53.refs_2_ = f32[256,256]{1,0:T(8,128)S(1)} collective-permute-done((f32[256,256]{1,0:T(8,128)S(1)}, f32[256,256]{1,0:T(8,128)S(1)}, u32[]{:S(2)}, u32[]{:S(2)}) %collective-permute-start.53) | collective-permute-done | bytes 262176 | tf_op jit(solution)/shard_map/ppermute | solution.py:78
  263.7 5.4 %collective-permute-done.54.refs_3_ = f32[256,256]{1,0:T(8,128)} collective-permute-done((f32[256,256]{1,0:T(8,128)S(1)}, f32[256,256]{1,0:T(8,128)}, u32[]{:S(2)}, u32[]{:S(2)}) %collective-permute-start.54) | collective-permute-done | bytes 262176 | tf_op jit(solution)/shard_map/ppermute | solution.py:78
  269.1 3.4 copy-done
  274.5 2.4 shard_map.72
  277.0 2.4 shard_map.73
  283.3 2.3 shard_map.77
  290.1 2.7 collective-permute-done.56
  295.7 3.2 collective-permute-done.57.refs_2_
  302.0 2.5 collective-permute-start.52
  305.9 3.0 collective-permute-done.52
  308.9 3.1 collective-permute-done.60
  317.3 10.1 %collective-permute-start.62 = (f32[512]{0:T(512)S(1)}, f32[512]{0:T(512)S(1)}, u32[]{:S(2)}, u32[]{:S(2)}) collective-permute-start(f32[512]{0:T(512)S(1)} %add.70), channel_id=1, source_target_pairs={{0,8},{4,12},{8,0},{12,4},{16,24},{20,28},{24,16},{28,20},{1,9},{5... | collective-permute-start | bytes 6152 | tf_op jit(solution)/shard_map/ppermute | solution.py:168
  328.9 8.8 %collective-permute-start.63 = (f32[512]{0:T(512)S(1)}, f32[512]{0:T(512)S(1)}, u32[]{:S(2)}, u32[]{:S(2)}) collective-permute-start(f32[512]{0:T(512)S(1)} %add.71), channel_id=1, source_target_pairs={{0,16},{4,20},{8,24},{12,28},{16,0},{20,4},{24,8},{28,12},{1,17},{... | collective-permute-start | bytes 6152 | tf_op jit(solution)/shard_map/ppermute | solution.py:168
  (214 shorter events, 101.0 us)
Async XLA Ops:
  7.2 40.0 %all-gather.11.cloned.1.call-start = ((), (), s32[]{:S(2)}) async-start(), calls=%async_computation | async-start | bytes 2621440 | tf_op jit(solution)/shard_map/all_gather | solution.py:126
  8.7 9.3 %collective-permute-start = (f32[1,256,256]{2,1,0:T(8,128)S(1)}, f32[1,256,256]{2,1,0:T(8,128)S(1)}, u32[]{:S(2)}, u32[]{:S(2)}) collective-permute-start(f32[1,256,256]{2,1,0:T(8,128)S(1)} %get-tuple-element.115), channel_id=1, source_target_pairs={{0,4},{4,0},{8,12},{12,8},{16,20},{20,16},{24,28},{28,24},{1,5},{5... | collective-permute-start | bytes 786440 | tf_op jit(solution)/shard_map/ppermute | solution.py:62
  12.7 8.7 %collective-permute-start.1 = (f32[256,256]{1,0:T(8,128)S(1)}, f32[256,256]{1,0:T(8,128)S(1)}, u32[]{:S(2)}, u32[]{:S(2)}) collective-permute-start(f32[256,256]{1,0:T(8,128)S(1)} %get-tuple-element.110.refs_1_), channel_id=1, source_target_pairs={{0,8},{4,12},{8,16},{12,20},{16,24},{20,28},{1,9},{5,13},{9,17},{1... | collective-permute-start | bytes 786440 | tf_op jit(solution)/shard_map/ppermute | solution.py:78
  22.3 81.5 %all-gather.15.cloned.1.call-start = ((), (), s32[]{:S(2)}) async-start(), calls=%async_computation.2 | async-start | bytes 2621440 | tf_op jit(solution)/shard_map/all_gather | solution.py:126
  22.3 8.8 %collective-permute-start.5 = (f32[256,256]{1,0:T(8,128)S(1)}, f32[256,256]{1,0:T(8,128)S(1)}, u32[]{:S(2)}, u32[]{:S(2)}) collective-permute-start(f32[256,256]{1,0:T(8,128)S(1)} %get-tuple-element.109.refs_1_), channel_id=1, source_target_pairs={{0,8},{4,12},{8,16},{12,20},{16,24},{20,28},{1,9},{5,13},{9,17},{1... | collective-permute-start | bytes 786440 | tf_op jit(solution)/shard_map/ppermute | solution.py:78
  31.8 6.4 %collective-permute-start.10 = (f32[1,256,256]{2,1,0:T(8,128)S(1)}, f32[1,256,256]{2,1,0:T(8,128)S(1)}, u32[]{:S(2)}, u32[]{:S(2)}) collective-permute-start(f32[1,256,256]{2,1,0:T(8,128)S(1)} %get-tuple-element.58), channel_id=1, source_target_pairs={{0,4},{4,0},{8,12},{12,8},{16,20},{20,16},{24,28},{28,24},{1,5},{5... | collective-permute-start | bytes 786440 | tf_op jit(solution)/shard_map/ppermute | solution.py:62
  39.0 110.1 %all-gather.13.cloned.1.call-start = ((), (), s32[]{:S(2)}) async-start(), calls=%async_computation.1 | async-start | bytes 2621440 | tf_op jit(solution)/shard_map/all_gather | solution.py:126
  39.8 6.4 %collective-permute-start.9 = (f32[1,256,256]{2,1,0:T(8,128)S(1)}, f32[1,256,256]{2,1,0:T(8,128)S(1)}, u32[]{:S(2)}, u32[]{:S(2)}) collective-permute-start(f32[1,256,256]{2,1,0:T(8,128)S(1)} %get-tuple-element.56), channel_id=1, source_target_pairs={{0,4},{4,0},{8,12},{12,8},{16,20},{20,16},{24,28},{28,24},{1,5},{5... | collective-permute-start | bytes 786440 | tf_op jit(solution)/shard_map/ppermute | solution.py:62
  47.1 146.8 %all-gather.17.cloned.1.call-start = ((), (), s32[]{:S(2)}) async-start(), calls=%async_computation.3 | async-start | bytes 7864320 | tf_op jit(solution)/shard_map/all_gather | solution.py:126
  49.8 9.3 %collective-permute-start.4 = (f32[256,256]{1,0:T(8,128)S(1)}, f32[256,256]{1,0:T(8,128)S(1)}, u32[]{:S(2)}, u32[]{:S(2)}) collective-permute-start(f32[256,256]{1,0:T(8,128)S(1)} %get-tuple-element.53), channel_id=1, source_target_pairs={{0,4},{4,0},{8,12},{12,8},{16,20},{20,16},{24,28},{28,24},{1,5},{5... | collective-permute-start | bytes 786440 | tf_op jit(solution)/shard_map/ppermute | solution.py:62
  51.8 11.3 %collective-permute-start.8 = (f32[256,256]{1,0:T(8,128)S(1)}, f32[256,256]{1,0:T(8,128)S(1)}, u32[]{:S(2)}, u32[]{:S(2)}) collective-permute-start(f32[256,256]{1,0:T(8,128)S(1)} %get-tuple-element.55), channel_id=1, source_target_pairs={{0,4},{4,0},{8,12},{12,8},{16,20},{20,16},{24,28},{28,24},{1,5},{5... | collective-permute-start | bytes 786440 | tf_op jit(solution)/shard_map/ppermute | solution.py:62
  63.2 39.1 %collective-permute-start.27 = (f32[3,256,256]{2,1,0:T(8,128)S(1)}, f32[3,256,256]{2,1,0:T(8,128)S(1)}, u32[]{:S(2)}, u32[]{:S(2)}) collective-permute-start(f32[3,256,256]{2,1,0:T(8,128)S(1)} %get-tuple-element.68), channel_id=1, source_target_pairs={{0,4},{4,0},{8,12},{12,8},{16,20},{20,16},{24,28},{28,24},{1,5},{5... | collective-permute-start | bytes 2359304 | tf_op jit(solution)/shard_map/ppermute | solution.py:62
  64.8 21.7 %collective-permute-start.11 = (f32[256,256]{1,0:T(8,128)S(1)}, f32[256,256]{1,0:T(8,128)S(1)}, u32[]{:S(2)}, u32[]{:S(2)}) collective-permute-start(f32[256,256]{1,0:T(8,128)S(1)} %add.56.refs_1_), channel_id=1, source_target_pairs={{0,8},{4,12},{8,16},{12,20},{16,24},{20,28},{24,0},{28,4},{1,9},{5... | collective-permute-start | bytes 786440 | tf_op jit(solution)/shard_map/ppermute | solution.py:78
  71.1 21.0 %collective-permute-start.19 = (f32[256,256]{1,0:T(8,128)S(1)}, f32[256,256]{1,0:T(8,128)S(1)}, u32[]{:S(2)}, u32[]{:S(2)}) collective-permute-start(f32[256,256]{1,0:T(8,128)S(1)} %add.57.refs_1_), channel_id=1, source_target_pairs={{0,8},{4,12},{8,16},{12,20},{16,24},{20,28},{24,0},{28,4},{1,9},{5... | collective-permute-start | bytes 786440 | tf_op jit(solution)/shard_map/ppermute | solution.py:78
  86.5 8.5 %collective-permute-start.12 = (f32[256,256]{1,0:T(8,128)S(1)}, f32[256,256]{1,0:T(8,128)S(1)}, u32[]{:S(2)}, u32[]{:S(2)}) collective-permute-start(f32[256,256]{1,0:T(8,128)S(1)} %collective-permute-done.11.refs_2_), channel_id=1, source_target_pairs={{0,8},{4,12},{8,16},{12,20},{16,24},{20,28},{24,0},{28,4},{1,9},{5... | collective-permute-start | bytes 786440 | tf_op jit(solution)/shard_map/ppermute | solution.py:78
  92.1 10.2 %collective-permute-start.20 = (f32[256,256]{1,0:T(8,128)S(1)}, f32[256,256]{1,0:T(8,128)S(1)}, u32[]{:S(2)}, u32[]{:S(2)}) collective-permute-start(f32[256,256]{1,0:T(8,128)S(1)} %collective-permute-done.19.refs_2_), channel_id=1, source_target_pairs={{0,8},{4,12},{8,16},{12,20},{16,24},{20,28},{24,0},{28,4},{1,9},{5... | collective-permute-start | bytes 786440 | tf_op jit(solution)/shard_map/ppermute | solution.py:78
  103.6 165.5 %all-gather.19.cloned.1.call-start = ((), (), s32[]{:S(2)}) async-start(), calls=%async_computation.4 | async-start | bytes 10485760 | tf_op jit(solution)/shard_map/all_gather | solution.py:126
  103.7 8.2 %collective-permute-start.13 = (f32[256,256]{1,0:T(8,128)S(1)}, f32[256,256]{1,0:T(8,128)S(1)}, u32[]{:S(2)}, u32[]{:S(2)}) collective-permute-start(f32[256,256]{1,0:T(8,128)S(1)} %collective-permute-done.12.refs_3_), channel_id=1, source_target_pairs={{0,8},{4,12},{8,16},{12,20},{16,24},{20,28},{24,0},{28,4},{1,9},{5... | collective-permute-start | bytes 786440 | tf_op jit(solution)/shard_map/ppermute | solution.py:78
  103.7 12.4 %collective-permute-start.21 = (f32[256,256]{1,0:T(8,128)S(1)}, f32[256,256]{1,0:T(8,128)S(1)}, u32[]{:S(2)}, u32[]{:S(2)}) collective-permute-start(f32[256,256]{1,0:T(8,128)S(1)} %collective-permute-done.20.refs_3_), channel_id=1, source_target_pairs={{0,8},{4,12},{8,16},{12,20},{16,24},{20,28},{24,0},{28,4},{1,9},{5... | collective-permute-start | bytes 786440 | tf_op jit(solution)/shard_map/ppermute | solution.py:78
  114.8 9.3 %collective-permute-start.14 = (f32[256,256]{1,0:T(8,128)S(1)}, f32[256,256]{1,0:T(8,128)S(1)}, u32[]{:S(2)}, u32[]{:S(2)}) collective-permute-start(f32[256,256]{1,0:T(8,128)S(1)} %get-tuple-element.61), channel_id=1, source_target_pairs={{0,4},{4,0},{8,12},{12,8},{16,20},{20,16},{24,28},{28,24},{1,5},{5... | collective-permute-start | bytes 786440 | tf_op jit(solution)/shard_map/ppermute | solution.py:62
  117.3 12.4 %collective-permute-start.22 = (f32[256,256]{1,0:T(8,128)S(1)}, f32[256,256]{1,0:T(8,128)S(1)}, u32[]{:S(2)}, u32[]{:S(2)}) collective-permute-start(f32[256,256]{1,0:T(8,128)S(1)} %get-tuple-element.65), channel_id=1, source_target_pairs={{0,4},{4,0},{8,12},{12,8},{16,20},{20,16},{24,28},{28,24},{1,5},{5... | collective-permute-start | bytes 786440 | tf_op jit(solution)/shard_map/ppermute | solution.py:62
  129.7 15.1 %collective-permute-start.44 = (f32[4,256,256]{2,1,0:T(8,128)S(1)}, f32[4,256,256]{2,1,0:T(8,128)S(1)}, u32[]{:S(2)}, u32[]{:S(2)}) collective-permute-start(f32[4,256,256]{2,1,0:T(8,128)S(1)} %get-tuple-element.82), channel_id=1, source_target_pairs={{0,4},{4,0},{8,12},{12,8},{16,20},{20,16},{24,28},{28,24},{1,5},{5... | collective-permute-start | bytes 3145736 | tf_op jit(solution)/shard_map/ppermute | solution.py:62
  132.4 6.7 %collective-permute-start.23 = (f32[256,256]{1,0:T(8,128)S(1)}, f32[256,256]{1,0:T(8,128)S(1)}, u32[]{:S(2)}, u32[]{:S(2)}) collective-permute-start(f32[256,256]{1,0:T(8,128)S(1)} %add.60.refs_1_), channel_id=1, source_target_pairs={{0,8},{4,12},{8,16},{12,20},{16,24},{20,28},{1,9},{5,13},{9,17},{1... | collective-permute-start | bytes 786440 | tf_op jit(solution)/shard_map/ppermute | solution.py:78
  147.8 7.1 %collective-permute-start.25 = (f32[256,256]{1,0:T(8,128)}, f32[256,256]{1,0:T(8,128)}, u32[]{:S(2)}, u32[]{:S(2)}) collective-permute-start(f32[256,256]{1,0:T(8,128)} %copy-done.19), channel_id=1, source_target_pairs={{16,24},{20,28},{17,25},{21,29},{18,26},{22,30},{19,27},{23,31}} | collective-permute-start | bytes 786440 | tf_op jit(solution)/shard_map/ppermute | solution.py:78
  153.8 6.4 %collective-permute-start.18 = (f32[256,256]{1,0:T(8,128)S(1)}, f32[256,256]{1,0:T(8,128)S(1)}, u32[]{:S(2)}, u32[]{:S(2)}) collective-permute-start(f32[256,256]{1,0:T(8,128)S(1)} %get-tuple-element.63), channel_id=1, source_target_pairs={{0,4},{4,0},{8,12},{12,8},{16,20},{20,16},{24,28},{28,24},{1,5},{5... | collective-permute-start | bytes 786440 | tf_op jit(solution)/shard_map/ppermute | solution.py:62
  156.9 7.0 %collective-permute-start.26 = (f32[256,256]{1,0:T(8,128)S(1)}, f32[256,256]{1,0:T(8,128)S(1)}, u32[]{:S(2)}, u32[]{:S(2)}) collective-permute-start(f32[256,256]{1,0:T(8,128)S(1)} %get-tuple-element.67), channel_id=1, source_target_pairs={{0,4},{4,0},{8,12},{12,8},{16,20},{20,16},{24,28},{28,24},{1,5},{5... | collective-permute-start | bytes 786440 | tf_op jit(solution)/shard_map/ppermute | solution.py:62
  160.2 22.1 %collective-permute-start.28 = (f32[256,256]{1,0:T(8,128)S(1)}, f32[256,256]{1,0:T(8,128)S(1)}, u32[]{:S(2)}, u32[]{:S(2)}) collective-permute-start(f32[256,256]{1,0:T(8,128)S(1)} %add.59.refs_1_), channel_id=1, source_target_pairs={{0,8},{4,12},{8,16},{12,20},{16,24},{20,28},{24,0},{28,4},{1,9},{5... | collective-permute-start | bytes 786440 | tf_op jit(solution)/shard_map/ppermute | solution.py:78
  163.9 21.7 %collective-permute-start.36 = (f32[256,256]{1,0:T(8,128)S(1)}, f32[256,256]{1,0:T(8,128)S(1)}, u32[]{:S(2)}, u32[]{:S(2)}) collective-permute-start(f32[256,256]{1,0:T(8,128)S(1)} %add.61.refs_1_), channel_id=1, source_target_pairs={{0,8},{4,12},{8,16},{12,20},{16,24},{20,28},{24,0},{28,4},{1,9},{5... | collective-permute-start | bytes 786440 | tf_op jit(solution)/shard_map/ppermute | solution.py:78
  182.3 8.3 %collective-permute-start.29 = (f32[256,256]{1,0:T(8,128)S(1)}, f32[256,256]{1,0:T(8,128)}, u32[]{:S(2)}, u32[]{:S(2)}) collective-permute-start(f32[256,256]{1,0:T(8,128)S(1)} %collective-permute-done.28.refs_2_), channel_id=1, source_target_pairs={{0,8},{4,12},{8,16},{12,20},{16,24},{20,28},{24,0},{28,4},{1,9},{5... | collective-permute-start | bytes 786440 | tf_op jit(solution)/shard_map/ppermute | solution.py:78
  185.7 8.2 %collective-permute-start.37 = (f32[256,256]{1,0:T(8,128)S(1)}, f32[256,256]{1,0:T(8,128)S(1)}, u32[]{:S(2)}, u32[]{:S(2)}) collective-permute-start(f32[256,256]{1,0:T(8,128)S(1)} %collective-permute-done.36.refs_2_), channel_id=1, source_target_pairs={{0,8},{4,12},{8,16},{12,20},{16,24},{20,28},{24,0},{28,4},{1,9},{5... | collective-permute-start | bytes 786440 | tf_op jit(solution)/shard_map/ppermute | solution.py:78
  190.6 8.5 %collective-permute-start.30 = (f32[256,256]{1,0:T(8,128)}, f32[256,256]{1,0:T(8,128)}, u32[]{:S(2)}, u32[]{:S(2)}) collective-permute-start(f32[256,256]{1,0:T(8,128)} %collective-permute-done.29.refs_3_), channel_id=1, source_target_pairs={{0,8},{4,12},{8,16},{12,20},{16,24},{20,28},{24,0},{28,4},{1,9},{5... | collective-permute-start | bytes 786440 | tf_op jit(solution)/shard_map/ppermute | solution.py:78
  193.8 10.0 %collective-permute-start.38 = (f32[256,256]{1,0:T(8,128)S(1)}, f32[256,256]{1,0:T(8,128)}, u32[]{:S(2)}, u32[]{:S(2)}) collective-permute-start(f32[256,256]{1,0:T(8,128)S(1)} %collective-permute-done.37.refs_3_), channel_id=1, source_target_pairs={{0,8},{4,12},{8,16},{12,20},{16,24},{20,28},{24,0},{28,4},{1,9},{5... | collective-permute-start | bytes 786440 | tf_op jit(solution)/shard_map/ppermute | solution.py:78
  201.5 9.2 %collective-permute-start.31 = (f32[256,256]{1,0:T(8,128)S(1)}, f32[256,256]{1,0:T(8,128)S(1)}, u32[]{:S(2)}, u32[]{:S(2)}) collective-permute-start(f32[256,256]{1,0:T(8,128)S(1)} %get-tuple-element.73), channel_id=1, source_target_pairs={{0,4},{4,0},{8,12},{12,8},{16,20},{20,16},{24,28},{28,24},{1,5},{5... | collective-permute-start | bytes 786440 | tf_op jit(solution)/shard_map/ppermute | solution.py:62
  206.1 9.5 %collective-permute-start.39 = (f32[256,256]{1,0:T(8,128)S(1)}, f32[256,256]{1,0:T(8,128)S(1)}, u32[]{:S(2)}, u32[]{:S(2)}) collective-permute-start(f32[256,256]{1,0:T(8,128)S(1)} %get-tuple-element.79), channel_id=1, source_target_pairs={{0,4},{4,0},{8,12},{12,8},{16,20},{20,16},{24,28},{28,24},{1,5},{5... | collective-permute-start | bytes 786440 | tf_op jit(solution)/shard_map/ppermute | solution.py:62
  215.6 8.0 %collective-permute-start.40 = (f32[256,256]{1,0:T(8,128)S(1)}, f32[256,256]{1,0:T(8,128)S(1)}, u32[]{:S(2)}, u32[]{:S(2)}) collective-permute-start(f32[256,256]{1,0:T(8,128)S(1)} %add.64.refs_1_), channel_id=1, source_target_pairs={{0,8},{4,12},{8,16},{12,20},{16,24},{20,28},{1,9},{5,13},{9,17},{1... | collective-permute-start | bytes 786440 | tf_op jit(solution)/shard_map/ppermute | solution.py:78
  216.9 7.3 %collective-permute-start.33 = (f32[256,256]{1,0:T(8,128)S(1)}, f32[256,256]{1,0:T(8,128)S(1)}, u32[]{:S(2)}, u32[]{:S(2)}) collective-permute-start(f32[256,256]{1,0:T(8,128)S(1)} %collective-permute-done.32.refs_2_), channel_id=1, source_target_pairs={{8,16},{12,20},{16,24},{20,28},{9,17},{13,21},{17,25},{21,29},{10,... | collective-permute-start | bytes 786440 | tf_op jit(solution)/shard_map/ppermute | solution.py:78
  228.4 14.0 %collective-permute-start.43 = (f32[256,256]{1,0:T(8,128)S(1)}, f32[256,256]{1,0:T(8,128)S(1)}, u32[]{:S(2)}, u32[]{:S(2)}) collective-permute-start(f32[256,256]{1,0:T(8,128)S(1)} %get-tuple-element.81), channel_id=1, source_target_pairs={{0,4},{4,0},{8,12},{12,8},{16,20},{20,16},{24,28},{28,24},{1,5},{5... | collective-permute-start | bytes 786440 | tf_op jit(solution)/shard_map/ppermute | solution.py:62
  233.2 22.0 %collective-permute-start.45 = (f32[256,256]{1,0:T(8,128)S(1)}, f32[256,256]{1,0:T(8,128)S(1)}, u32[]{:S(2)}, u32[]{:S(2)}) collective-permute-start(f32[256,256]{1,0:T(8,128)S(1)} %add.63.refs_1_), channel_id=1, source_target_pairs={{0,8},{4,12},{8,16},{12,20},{16,24},{20,28},{24,0},{28,4},{1,9},{5... | collective-permute-start | bytes 786440 | tf_op jit(solution)/shard_map/ppermute | solution.py:78
  242.4 18.4 %collective-permute-start.53 = (f32[256,256]{1,0:T(8,128)S(1)}, f32[256,256]{1,0:T(8,128)S(1)}, u32[]{:S(2)}, u32[]{:S(2)}) collective-permute-start(f32[256,256]{1,0:T(8,128)S(1)} %add.65.refs_1_), channel_id=1, source_target_pairs={{0,8},{4,12},{8,16},{12,20},{16,24},{20,28},{24,0},{28,4},{1,9},{5... | collective-permute-start | bytes 786440 | tf_op jit(solution)/shard_map/ppermute | solution.py:78
  255.2 8.5 %collective-permute-start.46 = (f32[256,256]{1,0:T(8,128)S(1)}, f32[256,256]{1,0:T(8,128)}, u32[]{:S(2)}, u32[]{:S(2)}) collective-permute-start(f32[256,256]{1,0:T(8,128)S(1)} %collective-permute-done.45.refs_2_), channel_id=1, source_target_pairs={{0,8},{4,12},{8,16},{12,20},{16,24},{20,28},{24,0},{28,4},{1,9},{5... | collective-permute-start | bytes 786440 | tf_op jit(solution)/shard_map/ppermute | solution.py:78
  260.8 8.3 %collective-permute-start.54 = (f32[256,256]{1,0:T(8,128)S(1)}, f32[256,256]{1,0:T(8,128)}, u32[]{:S(2)}, u32[]{:S(2)}) collective-permute-start(f32[256,256]{1,0:T(8,128)S(1)} %collective-permute-done.53.refs_2_), channel_id=1, source_target_pairs={{0,8},{4,12},{8,16},{12,20},{16,24},{20,28},{24,0},{28,4},{1,9},{5... | collective-permute-start | bytes 786440 | tf_op jit(solution)/shard_map/ppermute | solution.py:78
  263.7 13.2 %collective-permute-start.47 = (f32[256,256]{1,0:T(8,128)}, f32[256,256]{1,0:T(8,128)}, u32[]{:S(2)}, u32[]{:S(2)}) collective-permute-start(f32[256,256]{1,0:T(8,128)} %collective-permute-done.46.refs_3_), channel_id=1, source_target_pairs={{0,8},{4,12},{8,16},{12,20},{16,24},{20,28},{24,0},{28,4},{1,9},{5... | collective-permute-start | bytes 786440 | tf_op jit(solution)/shard_map/ppermute | solution.py:78
  269.1 14.2 %collective-permute-start.55 = (f32[256,256]{1,0:T(8,128)}, f32[256,256]{1,0:T(8,128)}, u32[]{:S(2)}, u32[]{:S(2)}) collective-permute-start(f32[256,256]{1,0:T(8,128)} %collective-permute-done.54.refs_3_), channel_id=1, source_target_pairs={{0,8},{4,12},{8,16},{12,20},{16,24},{20,28},{24,0},{28,4},{1,9},{5... | collective-permute-start | bytes 786440 | tf_op jit(solution)/shard_map/ppermute | solution.py:78
  279.4 9.3 %collective-permute-start.48 = (f32[256,256]{1,0:T(8,128)S(1)}, f32[256,256]{1,0:T(8,128)S(1)}, u32[]{:S(2)}, u32[]{:S(2)}) collective-permute-start(f32[256,256]{1,0:T(8,128)S(1)} %get-tuple-element.89), channel_id=1, source_target_pairs={{0,4},{4,0},{8,12},{12,8},{16,20},{20,16},{24,28},{28,24},{1,5},{5... | collective-permute-start | bytes 786440 | tf_op jit(solution)/shard_map/ppermute | solution.py:62
  285.5 7.3 %collective-permute-start.56 = (f32[256,256]{1,0:T(8,128)S(1)}, f32[256,256]{1,0:T(8,128)S(1)}, u32[]{:S(2)}, u32[]{:S(2)}) collective-permute-start(f32[256,256]{1,0:T(8,128)S(1)} %get-tuple-element.97), channel_id=1, source_target_pairs={{0,4},{4,0},{8,12},{12,8},{16,20},{20,16},{24,28},{28,24},{1,5},{5... | collective-permute-start | bytes 786440 | tf_op jit(solution)/shard_map/ppermute | solution.py:62
  302.0 6.9 %collective-permute-start.52 = (f32[256,256]{1,0:T(8,128)S(1)}, f32[256,256]{1,0:T(8,128)S(1)}, u32[]{:S(2)}, u32[]{:S(2)}) collective-permute-start(f32[256,256]{1,0:T(8,128)S(1)} %get-tuple-element.91), channel_id=1, source_target_pairs={{0,4},{4,0},{8,12},{12,8},{16,20},{20,16},{24,28},{28,24},{1,5},{5... | collective-permute-start | bytes 786440 | tf_op jit(solution)/shard_map/ppermute | solution.py:62
  317.3 11.6 %collective-permute-start.62 = (f32[512]{0:T(512)S(1)}, f32[512]{0:T(512)S(1)}, u32[]{:S(2)}, u32[]{:S(2)}) collective-permute-start(f32[512]{0:T(512)S(1)} %add.70), channel_id=1, source_target_pairs={{0,8},{4,12},{8,0},{12,4},{16,24},{20,28},{24,16},{28,20},{1,9},{5... | collective-permute-start | bytes 6152 | tf_op jit(solution)/shard_map/ppermute | solution.py:168
  328.9 10.3 %collective-permute-start.63 = (f32[512]{0:T(512)S(1)}, f32[512]{0:T(512)S(1)}, u32[]{:S(2)}, u32[]{:S(2)}) collective-permute-start(f32[512]{0:T(512)S(1)} %add.71), channel_id=1, source_target_pairs={{0,16},{4,20},{8,24},{12,28},{16,0},{20,4},{24,8},{28,12},{1,17},{... | collective-permute-start | bytes 6152 | tf_op jit(solution)/shard_map/ppermute | solution.py:168
  (53 other events, 200.6 us)
Sparse Core Ops, SparseCore 0:
  22.4 23.8 all-gather.10
  48.4 22.5 all-gather.14
  72.6 22.5 all-gather.12
  103.7 44.2 all-gather.16
  150.1 60.3 all-gather.18

commit v2 on v1

--- a/solution.py
+++ b/solution.py
@@ -158,15 +158,17 @@
             first_panels = panels
             slots, hops = ring_of(residuals, climb)
             if s == 0:
-                fetch([(3, 0), (3, 1), (3, 2), (3, 3)], hops[0], hops[2])
+                fetch([(3, 0), (3, 1), (3, 2), (3, 3)], hops[1], hops[3])
         solution = jnp.stack(
             [jnp.concatenate([solved[i][s] for i in range(streams)], axis=1) for s in range(segments)]
         )
-        totals = jnp.sum(solution * solution, axis=(0, 1))
-        bit = 1
-        while bit < rows:
+        totals = jnp.concatenate(
+            [sum(jnp.sum(panel * panel, axis=0) for panel in solved[i]) for i in range(streams)]
+        )
+        bit = rows // 2
+        while bit:
             totals = totals + lax.ppermute(totals, "row", [(r, r ^ bit) for r in range(rows)])
-            bit *= 2
+            bit //= 2
         variance = prior - totals / observed
         return (solution, variance)
 

time: 348 us -> 347 us (level)
  starting transfers between devices: 119 us -> 111 us
  local copies, waits for them, and re-layouts: 18.7 us -> 23.9 us
  waiting for transfers between devices: 152 us -> 156 us
    unnamed x60 -> x68, local copies, waits for them, and re-layouts: 17 us -> 22 us
    ppermute x42, starting transfers between devices: 75 us -> 69.9 us  [ring_of(): slots[i].append(lax.ppermute(value, 'row', route[hop - 1]))]
  transfers between devices with their start and end apart: 69 -> 69, of which waited for: 39 -> 37; matrix products, arithmetic and copies ran while one was open for 2% -> 3% of each run, Pallas kernels for 9% -> 8%
where the time goes in v2:
time: 347 us; the launch traced here: 346 us
  waiting for transfers between devices  156 us (45%)
  starting transfers between devices  111 us (32%)
  Pallas kernels  28.9 us (8%)
  local copies, waits for them, and re-layouts  23.9 us (7%)
  between operations  14.6 us (4%)
  other arithmetic  11.2 us (3%)
    ppermute x42, waiting for transfers between devices, ring_of(): slots[i].append(lax.ppermute(value, 'row', route[hop - 1]))  88.7 us
    ppermute x42, starting transfers between devices, ring_of(): slots[i].append(lax.ppermute(value, 'row', route[hop - 1]))  69.9 us
    ppermute x19, waiting for transfers between devices, swap(): return lax.ppermute(value, 'row', pair)  62.7 us
    pallas_call x20, Pallas kernels, product(): pl.pallas_call(functools.partial(product_kernel, layers, sign, len(pieces...  28.9 us
    ppermute x19, starting transfers between devices, swap(): return lax.ppermute(value, 'row', pair)  22.6 us
    unnamed x68, local copies, waits for them, and re-layouts  22 us
    ppermute x3, starting transfers between devices, body(): lax.ppermute(totals, 'row', [(r, r ^ bit) for r in range(rows)])  18.7 us
    another operation x9, other arithmetic, exchange(): return (jnp.stack([mine, after(got, *use)]), got)  8.14 us
  transfers between devices with their start and end apart: 69, of which 37 were waited for; matrix products, arithmetic and copies ran while one was open for 3% of the time, Pallas kernels for 8%

profile of v2, /device:TPU:0, one launch (start us, length us, event | category | flops | bytes accessed | tf_op | source)
XLA Modules:
  0.0 346.3 jit_solution(9686472392639197267)
XLA Ops:
  8.7 3.0 collective-permute-start
  12.7 3.5 %collective-permute-start.1 = (f32[256,256]{1,0:T(8,128)S(1)}, f32[256,256]{1,0:T(8,128)S(1)}, u32[]{:S(2)}, u32[]{:S(2)}) collective-permute-start(f32[256,256]{1,0:T(8,128)S(1)} %get-tuple-element.124.refs_1_), channel_id=1, source_target_pairs={{0,8},{4,12},{8,16},{12,20},{16,24},{20,28},{1,9},{5,13},{9,17},{1... | collective-permute-start | bytes 786440 | tf_op jit(solution)/shard_map/ppermute | solution.py:78
  18.0 3.4 collective-permute-done.1.refs_2_
  22.3 4.4 %collective-permute-start.5 = (f32[256,256]{1,0:T(8,128)S(1)}, f32[256,256]{1,0:T(8,128)S(1)}, u32[]{:S(2)}, u32[]{:S(2)}) collective-permute-start(f32[256,256]{1,0:T(8,128)S(1)} %get-tuple-element.123.refs_1_), channel_id=1, source_target_pairs={{0,8},{4,12},{8,16},{12,20},{16,24},{20,28},{1,9},{5,13},{9,17},{1... | collective-permute-start | bytes 786440 | tf_op jit(solution)/shard_map/ppermute | solution.py:78
  27.8 3.3 collective-permute-done.5.refs_2_
  33.3 4.9 %collective-permute-done.10 = f32[1,256,256]{2,1,0:T(8,128)S(1)} collective-permute-done((f32[1,256,256]{2,1,0:T(8,128)S(1)}, f32[1,256,256]{2,1,0:T(8,128)S(1)}, u32[]{:S(2)}, u32[]{:S(2)}) %collective-permute-start.10) | collective-permute-done | bytes 262176 | tf_op jit(solution)/shard_map/ppermute | solution.py:62
  41.4 4.9 %collective-permute-done.9 = f32[1,256,256]{2,1,0:T(8,128)S(1)} collective-permute-done((f32[1,256,256]{2,1,0:T(8,128)S(1)}, f32[1,256,256]{2,1,0:T(8,128)S(1)}, u32[]{:S(2)}, u32[]{:S(2)}) %collective-permute-start.9) | collective-permute-done | bytes 262176 | tf_op jit(solution)/shard_map/ppermute | solution.py:62
  54.1 5.0 %collective-permute-done.8 = f32[256,256]{1,0:T(8,128)S(1)} collective-permute-done((f32[256,256]{1,0:T(8,128)S(1)}, f32[256,256]{1,0:T(8,128)S(1)}, u32[]{:S(2)}, u32[]{:S(2)}) %collective-permute-start.8) | collective-permute-done | bytes 262176 | tf_op jit(solution)/shard_map/ppermute | solution.py:62
  59.2 3.9 %collective-permute-done.4 = f32[256,256]{1,0:T(8,128)S(1)} collective-permute-done((f32[256,256]{1,0:T(8,128)S(1)}, f32[256,256]{1,0:T(8,128)S(1)}, u32[]{:S(2)}, u32[]{:S(2)}) %collective-permute-start.4) | collective-permute-done | bytes 262176 | tf_op jit(solution)/shard_map/ppermute | solution.py:62
  64.8 6.4 %collective-permute-start.19 = (f32[256,256]{1,0:T(8,128)S(1)}, f32[256,256]{1,0:T(8,128)S(1)}, u32[]{:S(2)}, u32[]{:S(2)}) collective-permute-start(f32[256,256]{1,0:T(8,128)S(1)} %get-tuple-element.111.refs_1_), channel_id=1, source_target_pairs={{0,8},{4,12},{8,16},{12,20},{16,24},{20,28},{24,0},{28,4},{1,9},{5... | collective-permute-start | bytes 786440 | tf_op jit(solution)/shard_map/ppermute | solution.py:78
  71.2 6.9 %collective-permute-start.11 = (f32[256,256]{1,0:T(8,128)S(1)}, f32[256,256]{1,0:T(8,128)S(1)}, u32[]{:S(2)}, u32[]{:S(2)}) collective-permute-start(f32[256,256]{1,0:T(8,128)S(1)} %get-tuple-element.103.refs_1_), channel_id=1, source_target_pairs={{0,8},{4,12},{8,16},{12,20},{16,24},{20,28},{24,0},{28,4},{1,9},{5... | collective-permute-start | bytes 786440 | tf_op jit(solution)/shard_map/ppermute | solution.py:78
  78.1 8.5 %collective-permute-done.19.refs_2_ = f32[256,256]{1,0:T(8,128)S(1)} collective-permute-done((f32[256,256]{1,0:T(8,128)S(1)}, f32[256,256]{1,0:T(8,128)S(1)}, u32[]{:S(2)}, u32[]{:S(2)}) %collective-permute-start.19) | collective-permute-done | bytes 262176 | tf_op jit(solution)/shard_map/ppermute | solution.py:78
  86.6 5.3 %collective-permute-done.11.refs_2_ = f32[256,256]{1,0:T(8,128)S(1)} collective-permute-done((f32[256,256]{1,0:T(8,128)S(1)}, f32[256,256]{1,0:T(8,128)S(1)}, u32[]{:S(2)}, u32[]{:S(2)}) %collective-permute-start.11) | collective-permute-done | bytes 262176 | tf_op jit(solution)/shard_map/ppermute | solution.py:78
  91.9 2.8 collective-permute-done.20.refs_3_
  94.7 7.8 %collective-permute-done.12.refs_3_ = f32[256,256]{1,0:T(8,128)S(1)} collective-permute-done((f32[256,256]{1,0:T(8,128)S(1)}, f32[256,256]{1,0:T(8,128)S(1)}, u32[]{:S(2)}, u32[]{:S(2)}) %collective-permute-start.12) | collective-permute-done | bytes 262176 | tf_op jit(solution)/shard_map/ppermute | solution.py:78
  104.1 8.1 %collective-permute-done.21.refs_4_ = f32[256,256]{1,0:T(8,128)S(1)} collective-permute-done((f32[256,256]{1,0:T(8,128)S(1)}, f32[256,256]{1,0:T(8,128)S(1)}, u32[]{:S(2)}, u32[]{:S(2)}) %collective-permute-start.21) | collective-permute-done | bytes 262176 | tf_op jit(solution)/shard_map/ppermute | solution.py:78
  118.3 3.3 collective-permute-done.22
  123.1 4.1 %collective-permute-done.14 = f32[256,256]{1,0:T(8,128)S(1)} collective-permute-done((f32[256,256]{1,0:T(8,128)S(1)}, f32[256,256]{1,0:T(8,128)S(1)}, u32[]{:S(2)}, u32[]{:S(2)}) %collective-permute-start.14) | collective-permute-done | bytes 262176 | tf_op jit(solution)/shard_map/ppermute | solution.py:62
  128.8 3.6 %collective-permute-done.15.refs_2_ = f32[256,256]{1,0:T(8,128)S(1)} collective-permute-done((f32[256,256]{1,0:T(8,128)S(1)}, f32[256,256]{1,0:T(8,128)S(1)}, u32[]{:S(2)}, u32[]{:S(2)}) %collective-permute-start.15) | collective-permute-done | bytes 262176 | tf_op jit(solution)/shard_map/ppermute | solution.py:78
  139.1 10.7 %collective-permute-done.44 = f32[4,256,256]{2,1,0:T(8,128)S(1)} collective-permute-done((f32[4,256,256]{2,1,0:T(8,128)S(1)}, f32[4,256,256]{2,1,0:T(8,128)S(1)}, u32[]{:S(2)}, u32[]{:S(2)}) %collective-permute-start.44) | collective-permute-done | bytes 1048608 | tf_op jit(solution)/shard_map/ppermute | solution.py:62
  159.2 3.2 collective-permute-done.26
  162.4 3.5 %collective-permute-start.36 = (f32[256,256]{1,0:T(8,128)S(1)}, f32[256,256]{1,0:T(8,128)S(1)}, u32[]{:S(2)}, u32[]{:S(2)}) collective-permute-start(f32[256,256]{1,0:T(8,128)S(1)} %get-tuple-element.109.refs_1_), channel_id=1, source_target_pairs={{0,8},{4,12},{8,16},{12,20},{16,24},{20,28},{24,0},{28,4},{1,9},{5... | collective-permute-start | bytes 786440 | tf_op jit(solution)/shard_map/ppermute | solution.py:78
  166.0 4.9 %collective-permute-start.28 = (f32[256,256]{1,0:T(8,128)S(1)}, f32[256,256]{1,0:T(8,128)S(1)}, u32[]{:S(2)}, u32[]{:S(2)}) collective-permute-start(f32[256,256]{1,0:T(8,128)S(1)} %get-tuple-element.101.refs_1_), channel_id=1, source_target_pairs={{0,8},{4,12},{8,16},{12,20},{16,24},{20,28},{24,0},{28,4},{1,9},{5... | collective-permute-start | bytes 786440 | tf_op jit(solution)/shard_map/ppermute | solution.py:78
  170.9 8.3 %collective-permute-done.36.refs_2_ = f32[256,256]{1,0:T(8,128)S(1)} collective-permute-done((f32[256,256]{1,0:T(8,128)S(1)}, f32[256,256]{1,0:T(8,128)S(1)}, u32[]{:S(2)}, u32[]{:S(2)}) %collective-permute-start.36) | collective-permute-done | bytes 262176 | tf_op jit(solution)/shard_map/ppermute | solution.py:78
  179.9 4.6 %collective-permute-done.28.refs_2_ = f32[256,256]{1,0:T(8,128)S(1)} collective-permute-done((f32[256,256]{1,0:T(8,128)S(1)}, f32[256,256]{1,0:T(8,128)S(1)}, u32[]{:S(2)}, u32[]{:S(2)}) %collective-permute-start.28) | collective-permute-done | bytes 262176 | tf_op jit(solution)/shard_map/ppermute | solution.py:78
  184.5 3.0 collective-permute-done.37.refs_3_
  187.5 5.2 %collective-permute-done.29.refs_3_ = f32[256,256]{1,0:T(8,128)S(1)} collective-permute-done((f32[256,256]{1,0:T(8,128)S(1)}, f32[256,256]{1,0:T(8,128)S(1)}, u32[]{:S(2)}, u32[]{:S(2)}) %collective-permute-start.29) | collective-permute-done | bytes 262176 | tf_op jit(solution)/shard_map/ppermute | solution.py:78
  192.7 3.0 copy-done.1
  207.2 3.3 collective-permute-done.39
  211.8 4.3 %collective-permute-done.31 = f32[256,256]{1,0:T(8,128)S(1)} collective-permute-done((f32[256,256]{1,0:T(8,128)S(1)}, f32[256,256]{1,0:T(8,128)S(1)}, u32[]{:S(2)}, u32[]{:S(2)}) %collective-permute-start.31) | collective-permute-done | bytes 262176 | tf_op jit(solution)/shard_map/ppermute | solution.py:62
  218.2 4.1 %collective-permute-done.32.refs_2_ = f32[256,256]{1,0:T(8,128)S(1)} collective-permute-done((f32[256,256]{1,0:T(8,128)S(1)}, f32[256,256]{1,0:T(8,128)S(1)}, u32[]{:S(2)}, u32[]{:S(2)}) %collective-permute-start.32) | collective-permute-done | bytes 262176 | tf_op jit(solution)/shard_map/ppermute | solution.py:78
  228.7 3.2 collective-permute-done.43
  231.9 10.1 %collective-permute-start.53 = (f32[256,256]{1,0:T(8,128)S(1)}, f32[256,256]{1,0:T(8,128)S(1)}, u32[]{:S(2)}, u32[]{:S(2)}) collective-permute-start(f32[256,256]{1,0:T(8,128)S(1)} %get-tuple-element.113.refs_1_), channel_id=1, source_target_pairs={{0,8},{4,12},{8,16},{12,20},{16,24},{20,28},{24,0},{28,4},{1,9},{5... | collective-permute-start | bytes 786440 | tf_op jit(solution)/shard_map/ppermute | solution.py:78
  242.0 7.8 %collective-permute-start.45 = (f32[256,256]{1,0:T(8,128)S(1)}, f32[256,256]{1,0:T(8,128)S(1)}, u32[]{:S(2)}, u32[]{:S(2)}) collective-permute-start(f32[256,256]{1,0:T(8,128)S(1)} %get-tuple-element.105.refs_1_), channel_id=1, source_target_pairs={{0,8},{4,12},{8,16},{12,20},{16,24},{20,28},{24,0},{28,4},{1,9},{5... | collective-permute-start | bytes 786440 | tf_op jit(solution)/shard_map/ppermute | solution.py:78
  249.8 5.6 %collective-permute-done.53.refs_2_ = f32[256,256]{1,0:T(8,128)S(1)} collective-permute-done((f32[256,256]{1,0:T(8,128)S(1)}, f32[256,256]{1,0:T(8,128)S(1)}, u32[]{:S(2)}, u32[]{:S(2)}) %collective-permute-start.53) | collective-permute-done | bytes 262176 | tf_op jit(solution)/shard_map/ppermute | solution.py:78
  256.2 4.3 %collective-permute-done.45.refs_2_ = f32[256,256]{1,0:T(8,128)S(1)} collective-permute-done((f32[256,256]{1,0:T(8,128)S(1)}, f32[256,256]{1,0:T(8,128)S(1)}, u32[]{:S(2)}, u32[]{:S(2)}) %collective-permute-start.45) | collective-permute-done | bytes 262176 | tf_op jit(solution)/shard_map/ppermute | solution.py:78
  261.1 2.6 collective-permute-done.54.refs_3_
  263.7 5.0 %collective-permute-done.46.refs_3_ = f32[256,256]{1,0:T(8,128)} collective-permute-done((f32[256,256]{1,0:T(8,128)S(1)}, f32[256,256]{1,0:T(8,128)}, u32[]{:S(2)}, u32[]{:S(2)}) %collective-permute-start.46) | collective-permute-done | bytes 262176 | tf_op jit(solution)/shard_map/ppermute | solution.py:78
  268.7 3.4 copy-done
  274.2 2.5 shard_map.76
  284.0 2.3 shard_map.73
  289.9 2.8 collective-permute-done.48
  292.8 4.9 %collective-permute-start.49 = (f32[256,256]{1,0:T(8,128)S(1)}, f32[256,256]{1,0:T(8,128)S(1)}, u32[]{:S(2)}, u32[]{:S(2)}) collective-permute-start(f32[256,256]{1,0:T(8,128)S(1)} %add.84.refs_1_), channel_id=1, source_target_pairs={{0,8},{4,12},{8,16},{12,20},{16,24},{20,28},{1,9},{5,13},{9,17},{1... | collective-permute-start | bytes 786440 | tf_op jit(solution)/shard_map/ppermute | solution.py:78
  298.4 3.2 collective-permute-done.49.refs_2_
  308.1 3.1 collective-permute-done.60
  311.2 2.7 collective-permute-done.52
  314.1 15.9 %collective-permute-start.61 = (f32[512]{0:T(512)S(1)}, f32[512]{0:T(512)S(1)}, u32[]{:S(2)}, u32[]{:S(2)}) collective-permute-start(f32[512]{0:T(512)S(1)} %pad_maximum_fusion.8), channel_id=1, source_target_pairs={{0,16},{4,20},{8,24},{12,28},{16,0},{20,4},{24,8},{28,12},{1,17},{... | collective-permute-start | bytes 6152 | tf_op jit(solution)/shard_map/ppermute | solution.py:170
  331.5 2.5 collective-permute-start.62
  (223 shorter events, 98.8 us)
Async XLA Ops:
  7.2 40.0 %all-gather.11.cloned.1.call-start = ((), (), s32[]{:S(2)}) async-start(), calls=%async_computation | async-start | bytes 2621440 | tf_op jit(solution)/shard_map/all_gather | solution.py:126
  8.7 9.3 %collective-permute-start = (f32[1,256,256]{2,1,0:T(8,128)S(1)}, f32[1,256,256]{2,1,0:T(8,128)S(1)}, u32[]{:S(2)}, u32[]{:S(2)}) collective-permute-start(f32[1,256,256]{2,1,0:T(8,128)S(1)} %get-tuple-element.129), channel_id=1, source_target_pairs={{0,4},{4,0},{8,12},{12,8},{16,20},{20,16},{24,28},{28,24},{1,5},{5... | collective-permute-start | bytes 786440 | tf_op jit(solution)/shard_map/ppermute | solution.py:62
  12.7 8.7 %collective-permute-start.1 = (f32[256,256]{1,0:T(8,128)S(1)}, f32[256,256]{1,0:T(8,128)S(1)}, u32[]{:S(2)}, u32[]{:S(2)}) collective-permute-start(f32[256,256]{1,0:T(8,128)S(1)} %get-tuple-element.124.refs_1_), channel_id=1, source_target_pairs={{0,8},{4,12},{8,16},{12,20},{16,24},{20,28},{1,9},{5,13},{9,17},{1... | collective-permute-start | bytes 786440 | tf_op jit(solution)/shard_map/ppermute | solution.py:78
  22.3 81.9 %all-gather.15.cloned.1.call-start = ((), (), s32[]{:S(2)}) async-start(), calls=%async_computation.2 | async-start | bytes 2621440 | tf_op jit(solution)/shard_map/all_gather | solution.py:126
  22.3 8.8 %collective-permute-start.5 = (f32[256,256]{1,0:T(8,128)S(1)}, f32[256,256]{1,0:T(8,128)S(1)}, u32[]{:S(2)}, u32[]{:S(2)}) collective-permute-start(f32[256,256]{1,0:T(8,128)S(1)} %get-tuple-element.123.refs_1_), channel_id=1, source_target_pairs={{0,8},{4,12},{8,16},{12,20},{16,24},{20,28},{1,9},{5,13},{9,17},{1... | collective-permute-start | bytes 786440 | tf_op jit(solution)/shard_map/ppermute | solution.py:78
  31.7 6.4 %collective-permute-start.10 = (f32[1,256,256]{2,1,0:T(8,128)S(1)}, f32[1,256,256]{2,1,0:T(8,128)S(1)}, u32[]{:S(2)}, u32[]{:S(2)}) collective-permute-start(f32[1,256,256]{2,1,0:T(8,128)S(1)} %get-tuple-element.58), channel_id=1, source_target_pairs={{0,4},{4,0},{8,12},{12,8},{16,20},{20,16},{24,28},{28,24},{1,5},{5... | collective-permute-start | bytes 786440 | tf_op jit(solution)/shard_map/ppermute | solution.py:62
  39.0 112.3 %all-gather.13.cloned.1.call-start = ((), (), s32[]{:S(2)}) async-start(), calls=%async_computation.1 | async-start | bytes 2621440 | tf_op jit(solution)/shard_map/all_gather | solution.py:126
  39.8 6.4 %collective-permute-start.9 = (f32[1,256,256]{2,1,0:T(8,128)S(1)}, f32[1,256,256]{2,1,0:T(8,128)S(1)}, u32[]{:S(2)}, u32[]{:S(2)}) collective-permute-start(f32[1,256,256]{2,1,0:T(8,128)S(1)} %get-tuple-element.56), channel_id=1, source_target_pairs={{0,4},{4,0},{8,12},{12,8},{16,20},{20,16},{24,28},{28,24},{1,5},{5... | collective-permute-start | bytes 786440 | tf_op jit(solution)/shard_map/ppermute | solution.py:62
  47.1 145.6 %all-gather.17.cloned.1.call-start = ((), (), s32[]{:S(2)}) async-start(), calls=%async_computation.3 | async-start | bytes 7864320 | tf_op jit(solution)/shard_map/all_gather | solution.py:126
  49.8 9.3 %collective-permute-start.8 = (f32[256,256]{1,0:T(8,128)S(1)}, f32[256,256]{1,0:T(8,128)S(1)}, u32[]{:S(2)}, u32[]{:S(2)}) collective-permute-start(f32[256,256]{1,0:T(8,128)S(1)} %get-tuple-element.55), channel_id=1, source_target_pairs={{0,4},{4,0},{8,12},{12,8},{16,20},{20,16},{24,28},{28,24},{1,5},{5... | collective-permute-start | bytes 786440 | tf_op jit(solution)/shard_map/ppermute | solution.py:62
  52.7 10.4 %collective-permute-start.4 = (f32[256,256]{1,0:T(8,128)S(1)}, f32[256,256]{1,0:T(8,128)S(1)}, u32[]{:S(2)}, u32[]{:S(2)}) collective-permute-start(f32[256,256]{1,0:T(8,128)S(1)} %get-tuple-element.53), channel_id=1, source_target_pairs={{0,4},{4,0},{8,12},{12,8},{16,20},{20,16},{24,28},{28,24},{1,5},{5... | collective-permute-start | bytes 786440 | tf_op jit(solution)/shard_map/ppermute | solution.py:62
  63.2 39.4 %collective-permute-start.27 = (f32[3,256,256]{2,1,0:T(8,128)S(1)}, f32[3,256,256]{2,1,0:T(8,128)S(1)}, u32[]{:S(2)}, u32[]{:S(2)}) collective-permute-start(f32[3,256,256]{2,1,0:T(8,128)S(1)} %get-tuple-element.68), channel_id=1, source_target_pairs={{0,4},{4,0},{8,12},{12,8},{16,20},{20,16},{24,28},{28,24},{1,5},{5... | collective-permute-start | bytes 2359304 | tf_op jit(solution)/shard_map/ppermute | solution.py:62
  64.8 21.8 %collective-permute-start.19 = (f32[256,256]{1,0:T(8,128)S(1)}, f32[256,256]{1,0:T(8,128)S(1)}, u32[]{:S(2)}, u32[]{:S(2)}) collective-permute-start(f32[256,256]{1,0:T(8,128)S(1)} %get-tuple-element.111.refs_1_), channel_id=1, source_target_pairs={{0,8},{4,12},{8,16},{12,20},{16,24},{20,28},{24,0},{28,4},{1,9},{5... | collective-permute-start | bytes 786440 | tf_op jit(solution)/shard_map/ppermute | solution.py:78
  71.2 20.8 %collective-permute-start.11 = (f32[256,256]{1,0:T(8,128)S(1)}, f32[256,256]{1,0:T(8,128)S(1)}, u32[]{:S(2)}, u32[]{:S(2)}) collective-permute-start(f32[256,256]{1,0:T(8,128)S(1)} %get-tuple-element.103.refs_1_), channel_id=1, source_target_pairs={{0,8},{4,12},{8,16},{12,20},{16,24},{20,28},{24,0},{28,4},{1,9},{5... | collective-permute-start | bytes 786440 | tf_op jit(solution)/shard_map/ppermute | solution.py:78
  86.6 8.2 %collective-permute-start.20 = (f32[256,256]{1,0:T(8,128)S(1)}, f32[256,256]{1,0:T(8,128)S(1)}, u32[]{:S(2)}, u32[]{:S(2)}) collective-permute-start(f32[256,256]{1,0:T(8,128)S(1)} %collective-permute-done.19.refs_2_), channel_id=1, source_target_pairs={{0,8},{4,12},{8,16},{12,20},{16,24},{20,28},{24,0},{28,4},{1,9},{5... | collective-permute-start | bytes 786440 | tf_op jit(solution)/shard_map/ppermute | solution.py:78
  91.9 10.7 %collective-permute-start.12 = (f32[256,256]{1,0:T(8,128)S(1)}, f32[256,256]{1,0:T(8,128)S(1)}, u32[]{:S(2)}, u32[]{:S(2)}) collective-permute-start(f32[256,256]{1,0:T(8,128)S(1)} %collective-permute-done.11.refs_2_), channel_id=1, source_target_pairs={{0,8},{4,12},{8,16},{12,20},{16,24},{20,28},{24,0},{28,4},{1,9},{5... | collective-permute-start | bytes 786440 | tf_op jit(solution)/shard_map/ppermute | solution.py:78
  103.9 164.8 %all-gather.19.cloned.1.call-start = ((), (), s32[]{:S(2)}) async-start(), calls=%async_computation.4 | async-start | bytes 10485760 | tf_op jit(solution)/shard_map/all_gather | solution.py:126
  104.0 8.2 %collective-permute-start.21 = (f32[256,256]{1,0:T(8,128)S(1)}, f32[256,256]{1,0:T(8,128)S(1)}, u32[]{:S(2)}, u32[]{:S(2)}) collective-permute-start(f32[256,256]{1,0:T(8,128)S(1)} %collective-permute-done.20.refs_3_), channel_id=1, source_target_pairs={{0,8},{4,12},{8,16},{12,20},{16,24},{20,28},{24,0},{28,4},{1,9},{5... | collective-permute-start | bytes 786440 | tf_op jit(solution)/shard_map/ppermute | solution.py:78
  104.0 12.2 %collective-permute-start.13 = (f32[256,256]{1,0:T(8,128)S(1)}, f32[256,256]{1,0:T(8,128)S(1)}, u32[]{:S(2)}, u32[]{:S(2)}) collective-permute-start(f32[256,256]{1,0:T(8,128)S(1)} %collective-permute-done.12.refs_3_), channel_id=1, source_target_pairs={{0,8},{4,12},{8,16},{12,20},{16,24},{20,28},{24,0},{28,4},{1,9},{5... | collective-permute-start | bytes 786440 | tf_op jit(solution)/shard_map/ppermute | solution.py:78
  115.0 6.5 %collective-permute-start.22 = (f32[256,256]{1,0:T(8,128)S(1)}, f32[256,256]{1,0:T(8,128)S(1)}, u32[]{:S(2)}, u32[]{:S(2)}) collective-permute-start(f32[256,256]{1,0:T(8,128)S(1)} %get-tuple-element.65), channel_id=1, source_target_pairs={{0,4},{4,0},{8,12},{12,8},{16,20},{20,16},{24,28},{28,24},{1,5},{5... | collective-permute-start | bytes 786440 | tf_op jit(solution)/shard_map/ppermute | solution.py:62
  117.3 9.9 %collective-permute-start.14 = (f32[256,256]{1,0:T(8,128)S(1)}, f32[256,256]{1,0:T(8,128)S(1)}, u32[]{:S(2)}, u32[]{:S(2)}) collective-permute-start(f32[256,256]{1,0:T(8,128)S(1)} %get-tuple-element.61), channel_id=1, source_target_pairs={{0,4},{4,0},{8,12},{12,8},{16,20},{20,16},{24,28},{28,24},{1,5},{5... | collective-permute-start | bytes 786440 | tf_op jit(solution)/shard_map/ppermute | solution.py:62
  121.6 7.1 %collective-permute-start.23 = (f32[256,256]{1,0:T(8,128)S(1)}, f32[256,256]{1,0:T(8,128)S(1)}, u32[]{:S(2)}, u32[]{:S(2)}) collective-permute-start(f32[256,256]{1,0:T(8,128)S(1)} %add.78.refs_1_), channel_id=1, source_target_pairs={{0,8},{4,12},{8,16},{12,20},{16,24},{20,28},{1,9},{5,13},{9,17},{1... | collective-permute-start | bytes 786440 | tf_op jit(solution)/shard_map/ppermute | solution.py:78
  132.4 17.4 %collective-permute-start.44 = (f32[4,256,256]{2,1,0:T(8,128)S(1)}, f32[4,256,256]{2,1,0:T(8,128)S(1)}, u32[]{:S(2)}, u32[]{:S(2)}) collective-permute-start(f32[4,256,256]{2,1,0:T(8,128)S(1)} %get-tuple-element.82), channel_id=1, source_target_pairs={{0,4},{4,0},{8,12},{12,8},{16,20},{20,16},{24,28},{28,24},{1,5},{5... | collective-permute-start | bytes 3145736 | tf_op jit(solution)/shard_map/ppermute | solution.py:62
  155.9 6.4 %collective-permute-start.26 = (f32[256,256]{1,0:T(8,128)S(1)}, f32[256,256]{1,0:T(8,128)S(1)}, u32[]{:S(2)}, u32[]{:S(2)}) collective-permute-start(f32[256,256]{1,0:T(8,128)S(1)} %get-tuple-element.67), channel_id=1, source_target_pairs={{0,4},{4,0},{8,12},{12,8},{16,20},{20,16},{24,28},{28,24},{1,5},{5... | collective-permute-start | bytes 786440 | tf_op jit(solution)/shard_map/ppermute | solution.py:62
  158.2 7.8 %collective-permute-start.18 = (f32[256,256]{1,0:T(8,128)S(1)}, f32[256,256]{1,0:T(8,128)S(1)}, u32[]{:S(2)}, u32[]{:S(2)}) collective-permute-start(f32[256,256]{1,0:T(8,128)S(1)} %get-tuple-element.63), channel_id=1, source_target_pairs={{0,4},{4,0},{8,12},{12,8},{16,20},{20,16},{24,28},{28,24},{1,5},{5... | collective-permute-start | bytes 786440 | tf_op jit(solution)/shard_map/ppermute | solution.py:62
  162.4 16.8 %collective-permute-start.36 = (f32[256,256]{1,0:T(8,128)S(1)}, f32[256,256]{1,0:T(8,128)S(1)}, u32[]{:S(2)}, u32[]{:S(2)}) collective-permute-start(f32[256,256]{1,0:T(8,128)S(1)} %get-tuple-element.109.refs_1_), channel_id=1, source_target_pairs={{0,8},{4,12},{8,16},{12,20},{16,24},{20,28},{24,0},{28,4},{1,9},{5... | collective-permute-start | bytes 786440 | tf_op jit(solution)/shard_map/ppermute | solution.py:78
  166.0 18.5 %collective-permute-start.28 = (f32[256,256]{1,0:T(8,128)S(1)}, f32[256,256]{1,0:T(8,128)S(1)}, u32[]{:S(2)}, u32[]{:S(2)}) collective-permute-start(f32[256,256]{1,0:T(8,128)S(1)} %get-tuple-element.101.refs_1_), channel_id=1, source_target_pairs={{0,8},{4,12},{8,16},{12,20},{16,24},{20,28},{24,0},{28,4},{1,9},{5... | collective-permute-start | bytes 786440 | tf_op jit(solution)/shard_map/ppermute | solution.py:78
  179.2 8.3 %collective-permute-start.37 = (f32[256,256]{1,0:T(8,128)S(1)}, f32[256,256]{1,0:T(8,128)}, u32[]{:S(2)}, u32[]{:S(2)}) collective-permute-start(f32[256,256]{1,0:T(8,128)S(1)} %collective-permute-done.36.refs_2_), channel_id=1, source_target_pairs={{0,8},{4,12},{8,16},{12,20},{16,24},{20,28},{24,0},{28,4},{1,9},{5... | collective-permute-start | bytes 786440 | tf_op jit(solution)/shard_map/ppermute | solution.py:78
  184.5 8.2 %collective-permute-start.29 = (f32[256,256]{1,0:T(8,128)S(1)}, f32[256,256]{1,0:T(8,128)S(1)}, u32[]{:S(2)}, u32[]{:S(2)}) collective-permute-start(f32[256,256]{1,0:T(8,128)S(1)} %collective-permute-done.28.refs_2_), channel_id=1, source_target_pairs={{0,8},{4,12},{8,16},{12,20},{16,24},{20,28},{24,0},{28,4},{1,9},{5... | collective-permute-start | bytes 786440 | tf_op jit(solution)/shard_map/ppermute | solution.py:78
  187.5 10.2 %collective-permute-start.38 = (f32[256,256]{1,0:T(8,128)}, f32[256,256]{1,0:T(8,128)}, u32[]{:S(2)}, u32[]{:S(2)}) collective-permute-start(f32[256,256]{1,0:T(8,128)} %collective-permute-done.37.refs_3_), channel_id=1, source_target_pairs={{0,8},{4,12},{8,16},{12,20},{16,24},{20,28},{24,0},{28,4},{1,9},{5... | collective-permute-start | bytes 786440 | tf_op jit(solution)/shard_map/ppermute | solution.py:78
  192.7 11.0 %collective-permute-start.30 = (f32[256,256]{1,0:T(8,128)S(1)}, f32[256,256]{1,0:T(8,128)}, u32[]{:S(2)}, u32[]{:S(2)}) collective-permute-start(f32[256,256]{1,0:T(8,128)S(1)} %collective-permute-done.29.refs_3_), channel_id=1, source_target_pairs={{0,8},{4,12},{8,16},{12,20},{16,24},{20,28},{24,0},{28,4},{1,9},{5... | collective-permute-start | bytes 786440 | tf_op jit(solution)/shard_map/ppermute | solution.py:78
  201.7 8.8 %collective-permute-start.39 = (f32[256,256]{1,0:T(8,128)S(1)}, f32[256,256]{1,0:T(8,128)S(1)}, u32[]{:S(2)}, u32[]{:S(2)}) collective-permute-start(f32[256,256]{1,0:T(8,128)S(1)} %get-tuple-element.79), channel_id=1, source_target_pairs={{0,4},{4,0},{8,12},{12,8},{16,20},{20,16},{24,28},{28,24},{1,5},{5... | collective-permute-start | bytes 786440 | tf_op jit(solution)/shard_map/ppermute | solution.py:62
  205.9 10.2 %collective-permute-start.31 = (f32[256,256]{1,0:T(8,128)S(1)}, f32[256,256]{1,0:T(8,128)S(1)}, u32[]{:S(2)}, u32[]{:S(2)}) collective-permute-start(f32[256,256]{1,0:T(8,128)S(1)} %get-tuple-element.73), channel_id=1, source_target_pairs={{0,4},{4,0},{8,12},{12,8},{16,20},{20,16},{24,28},{28,24},{1,5},{5... | collective-permute-start | bytes 786440 | tf_op jit(solution)/shard_map/ppermute | solution.py:62
  210.5 6.9 %collective-permute-start.40 = (f32[256,256]{1,0:T(8,128)S(1)}, f32[256,256]{1,0:T(8,128)S(1)}, u32[]{:S(2)}, u32[]{:S(2)}) collective-permute-start(f32[256,256]{1,0:T(8,128)S(1)} %add.82.refs_1_), channel_id=1, source_target_pairs={{0,8},{4,12},{8,16},{12,20},{16,24},{20,28},{1,9},{5,13},{9,17},{1... | collective-permute-start | bytes 786440 | tf_op jit(solution)/shard_map/ppermute | solution.py:78
  225.4 6.4 %collective-permute-start.43 = (f32[256,256]{1,0:T(8,128)S(1)}, f32[256,256]{1,0:T(8,128)S(1)}, u32[]{:S(2)}, u32[]{:S(2)}) collective-permute-start(f32[256,256]{1,0:T(8,128)S(1)} %get-tuple-element.81), channel_id=1, source_target_pairs={{0,4},{4,0},{8,12},{12,8},{16,20},{20,16},{24,28},{28,24},{1,5},{5... | collective-permute-start | bytes 786440 | tf_op jit(solution)/shard_map/ppermute | solution.py:62
  226.7 15.2 %collective-permute-start.35 = (f32[256,256]{1,0:T(8,128)S(1)}, f32[256,256]{1,0:T(8,128)S(1)}, u32[]{:S(2)}, u32[]{:S(2)}) collective-permute-start(f32[256,256]{1,0:T(8,128)S(1)} %get-tuple-element.75), channel_id=1, source_target_pairs={{0,4},{4,0},{8,12},{12,8},{16,20},{20,16},{24,28},{28,24},{1,5},{5... | collective-permute-start | bytes 786440 | tf_op jit(solution)/shard_map/ppermute | solution.py:62
  231.9 23.5 %collective-permute-start.53 = (f32[256,256]{1,0:T(8,128)S(1)}, f32[256,256]{1,0:T(8,128)S(1)}, u32[]{:S(2)}, u32[]{:S(2)}) collective-permute-start(f32[256,256]{1,0:T(8,128)S(1)} %get-tuple-element.113.refs_1_), channel_id=1, source_target_pairs={{0,8},{4,12},{8,16},{12,20},{16,24},{20,28},{24,0},{28,4},{1,9},{5... | collective-permute-start | bytes 786440 | tf_op jit(solution)/shard_map/ppermute | solution.py:78
  242.0 18.4 %collective-permute-start.45 = (f32[256,256]{1,0:T(8,128)S(1)}, f32[256,256]{1,0:T(8,128)S(1)}, u32[]{:S(2)}, u32[]{:S(2)}) collective-permute-start(f32[256,256]{1,0:T(8,128)S(1)} %get-tuple-element.105.refs_1_), channel_id=1, source_target_pairs={{0,8},{4,12},{8,16},{12,20},{16,24},{20,28},{24,0},{28,4},{1,9},{5... | collective-permute-start | bytes 786440 | tf_op jit(solution)/shard_map/ppermute | solution.py:78
  255.4 8.3 %collective-permute-start.54 = (f32[256,256]{1,0:T(8,128)S(1)}, f32[256,256]{1,0:T(8,128)}, u32[]{:S(2)}, u32[]{:S(2)}) collective-permute-start(f32[256,256]{1,0:T(8,128)S(1)} %collective-permute-done.53.refs_2_), channel_id=1, source_target_pairs={{0,8},{4,12},{8,16},{12,20},{16,24},{20,28},{24,0},{28,4},{1,9},{5... | collective-permute-start | bytes 786440 | tf_op jit(solution)/shard_map/ppermute | solution.py:78
  260.4 8.3 %collective-permute-start.46 = (f32[256,256]{1,0:T(8,128)S(1)}, f32[256,256]{1,0:T(8,128)}, u32[]{:S(2)}, u32[]{:S(2)}) collective-permute-start(f32[256,256]{1,0:T(8,128)S(1)} %collective-permute-done.45.refs_2_), channel_id=1, source_target_pairs={{0,8},{4,12},{8,16},{12,20},{16,24},{20,28},{24,0},{28,4},{1,9},{5... | collective-permute-start | bytes 786440 | tf_op jit(solution)/shard_map/ppermute | solution.py:78
  263.7 13.0 %collective-permute-start.55 = (f32[256,256]{1,0:T(8,128)}, f32[256,256]{1,0:T(8,128)}, u32[]{:S(2)}, u32[]{:S(2)}) collective-permute-start(f32[256,256]{1,0:T(8,128)} %collective-permute-done.54.refs_3_), channel_id=1, source_target_pairs={{0,8},{4,12},{8,16},{12,20},{16,24},{20,28},{24,0},{28,4},{1,9},{5... | collective-permute-start | bytes 786440 | tf_op jit(solution)/shard_map/ppermute | solution.py:78
  268.7 15.3 %collective-permute-start.47 = (f32[256,256]{1,0:T(8,128)}, f32[256,256]{1,0:T(8,128)}, u32[]{:S(2)}, u32[]{:S(2)}) collective-permute-start(f32[256,256]{1,0:T(8,128)} %collective-permute-done.46.refs_3_), channel_id=1, source_target_pairs={{0,8},{4,12},{8,16},{12,20},{16,24},{20,28},{24,0},{28,4},{1,9},{5... | collective-permute-start | bytes 786440 | tf_op jit(solution)/shard_map/ppermute | solution.py:78
  279.2 9.3 %collective-permute-start.56 = (f32[256,256]{1,0:T(8,128)S(1)}, f32[256,256]{1,0:T(8,128)S(1)}, u32[]{:S(2)}, u32[]{:S(2)}) collective-permute-start(f32[256,256]{1,0:T(8,128)S(1)} %get-tuple-element.97), channel_id=1, source_target_pairs={{0,4},{4,0},{8,12},{12,8},{16,20},{20,16},{24,28},{28,24},{1,5},{5... | collective-permute-start | bytes 786440 | tf_op jit(solution)/shard_map/ppermute | solution.py:62
  286.3 6.4 %collective-permute-start.48 = (f32[256,256]{1,0:T(8,128)S(1)}, f32[256,256]{1,0:T(8,128)S(1)}, u32[]{:S(2)}, u32[]{:S(2)}) collective-permute-start(f32[256,256]{1,0:T(8,128)S(1)} %get-tuple-element.89), channel_id=1, source_target_pairs={{0,4},{4,0},{8,12},{12,8},{16,20},{20,16},{24,28},{28,24},{1,5},{5... | collective-permute-start | bytes 786440 | tf_op jit(solution)/shard_map/ppermute | solution.py:62
  288.6 9.1 %collective-permute-start.57 = (f32[256,256]{1,0:T(8,128)S(1)}, f32[256,256]{1,0:T(8,128)S(1)}, u32[]{:S(2)}, u32[]{:S(2)}) collective-permute-start(f32[256,256]{1,0:T(8,128)S(1)} %add.86.refs_1_), channel_id=1, source_target_pairs={{0,8},{4,12},{8,16},{12,20},{16,24},{20,28},{1,9},{5,13},{9,17},{1... | collective-permute-start | bytes 786440 | tf_op jit(solution)/shard_map/ppermute | solution.py:78
  292.8 8.8 %collective-permute-start.49 = (f32[256,256]{1,0:T(8,128)S(1)}, f32[256,256]{1,0:T(8,128)S(1)}, u32[]{:S(2)}, u32[]{:S(2)}) collective-permute-start(f32[256,256]{1,0:T(8,128)S(1)} %add.84.refs_1_), channel_id=1, source_target_pairs={{0,8},{4,12},{8,16},{12,20},{16,24},{20,28},{1,9},{5,13},{9,17},{1... | collective-permute-start | bytes 786440 | tf_op jit(solution)/shard_map/ppermute | solution.py:78
  306.1 7.9 %collective-permute-start.52 = (f32[256,256]{1,0:T(8,128)S(1)}, f32[256,256]{1,0:T(8,128)S(1)}, u32[]{:S(2)}, u32[]{:S(2)}) collective-permute-start(f32[256,256]{1,0:T(8,128)S(1)} %get-tuple-element.91), channel_id=1, source_target_pairs={{0,4},{4,0},{8,12},{12,8},{16,20},{20,16},{24,28},{28,24},{1,5},{5... | collective-permute-start | bytes 786440 | tf_op jit(solution)/shard_map/ppermute | solution.py:62
  314.1 17.5 %collective-permute-start.61 = (f32[512]{0:T(512)S(1)}, f32[512]{0:T(512)S(1)}, u32[]{:S(2)}, u32[]{:S(2)}) collective-permute-start(f32[512]{0:T(512)S(1)} %pad_maximum_fusion.8), channel_id=1, source_target_pairs={{0,16},{4,20},{8,24},{12,28},{16,0},{20,4},{24,8},{28,12},{1,17},{... | collective-permute-start | bytes 6152 | tf_op jit(solution)/shard_map/ppermute | solution.py:170
  (57 other events, 173.6 us)
Sparse Core Ops, SparseCore 0:
  22.4 23.8 all-gather.10
  47.9 22.5 all-gather.14
  72.1 22.5 all-gather.12
  104.0 44.0 all-gather.16
  151.4 65.0 all-gather.18
